TPU v7x, 128 devices: a whole 4x4x4 slice. The times are simulated.
128 devices in a mesh: blk: 16 (over z, x_hi, core), fiber: 8 (over x_lo, y).
Axes of the slice: x: 4 (x_hi: 2, x_lo: 2; x = x_hi * 2 + x_lo), y: 4, z: 4, core: 2. Of those that a mesh axis runs over, the one named last changes fastest.
Arguments:
- embedding: bfloat16 [65536, 256], P(('blk', 'fiber')), may hold values from -2.09375 to 2.09375
- tile_dest: int32 [16, 8, 16, 24], P('blk', 'fiber'), may hold values from 0 to 31, as said below
- tile_source: int32 [16, 8, 16, 24], P('blk', 'fiber'), may hold values from 0 to 3
- tile_count: int32 [16, 8, 16], P('blk', 'fiber'), may hold values from 2 to 24, as said below
- pattern_id: int32 [16, 8, 16, 24], P('blk', 'fiber'), may hold values from 0 to 63
- pattern_bank: int32 [64, 4, 128], replicated, may hold values from -2147483648 to 2147483646
- negative_dest: int32 [16, 8, 16, 4], P('blk', 'fiber'), may hold values from 0 to 31
- negative_source: int32 [16, 8, 16, 4], P('blk', 'fiber'), may hold values from 0 to 3
Outputs:
- gradient: float32 [65536, 256], P(('blk', 'fiber'))
Inputs may be any that keep to these rules, and one draw needn't show every extreme that they name: At each block, fiber and stop the 24 pairs (tile_dest, tile_source) are distinct. `tile_count`: slots at or past the count are unused; some block, fiber and stop lists 24 tiles.
All inputs are finite; a program needn't handle non-finite values.
Results may differ from a plain program's by a relative error of at most 0.00064.
Values may be sent and summed in bfloat16 or wider, within the bound.
A program may use at most 64 MiB of HBM per device.

v0:
```python
import math

import jax
import jax.numpy as jnp
from jax import lax
from jax.sharding import PartitionSpec as P


def from_behind(shard, axis, by):
    devices = lax.axis_size(axis)
    return lax.ppermute(shard, axis, [(i, (i + by) % devices) for i in range(devices)])


def unpack_bits(packed_words):
    shifts = jnp.arange(32, dtype=jnp.int32)
    bit_values = jnp.right_shift(packed_words[:, :, None, :], shifts[None, None, :, None]) & 1
    flat_bits = bit_values.reshape(
        packed_words.shape[0], packed_words.shape[1] * 32, packed_words.shape[2]
    )
    return flat_bits.astype(jnp.float32)


def one_hot_rows(index_list, table_size):
    return index_list[:, None] == jnp.arange(table_size, dtype=jnp.int32)[None, :]


def tile_terms(totals, dest_tiles, source_tiles, dest_ids, source_ids, mask_bits, live_slots):
    dest_sum, source_sum = totals
    dest_pick = one_hot_rows(dest_ids, dest_tiles.shape[0])
    source_pick = one_hot_rows(source_ids, source_tiles.shape[0])
    dest_rows = jnp.einsum(
        "gp,pid->gid",
        dest_pick.astype(jnp.bfloat16),
        dest_tiles,
        preferred_element_type=jnp.float32,
    ).astype(jnp.bfloat16)
    source_rows = jnp.einsum(
        "gp,pjd->gjd",
        source_pick.astype(jnp.bfloat16),
        source_tiles,
        preferred_element_type=jnp.float32,
    ).astype(jnp.bfloat16)
    scores = jnp.einsum("gjd,gid->gji", source_rows, dest_rows, preferred_element_type=jnp.float32)
    residual = (live_slots[:, None, None] * (mask_bits - jax.nn.sigmoid(scores))).astype(
        jnp.bfloat16
    )
    to_dest = jnp.einsum("gji,gjd->gid", residual, source_rows, preferred_element_type=jnp.float32)
    to_source = jnp.einsum("gji,gid->gjd", residual, dest_rows, preferred_element_type=jnp.float32)
    dest_sum = dest_sum + jnp.einsum(
        "gp,gid->pid", dest_pick.astype(jnp.float32), to_dest, precision=lax.Precision.HIGHEST
    )
    source_sum = source_sum + jnp.einsum(
        "gp,gjd->pjd", source_pick.astype(jnp.float32), to_source, precision=lax.Precision.HIGHEST
    )
    return (dest_sum, source_sum)


def visit_stop(stop_index, totals, dest_tiles, source_tiles, tables, pattern_bank):
    dest_lists, source_lists, count_lists, pattern_lists, negative_dests, negative_sources = tables
    tile_size = dest_tiles.shape[1]
    negative_total = negative_dests.shape[1]
    totals = tile_terms(
        totals,
        dest_tiles,
        source_tiles,
        negative_dests[stop_index],
        negative_sources[stop_index],
        jnp.zeros((negative_total, tile_size, tile_size), jnp.float32),
        jnp.ones((negative_total,), jnp.float32),
    )
    capacity = dest_lists.shape[1]
    group_size = math.gcd(capacity, 8)
    listed_count = count_lists[stop_index]
    dest_line = dest_lists[stop_index]
    source_line = source_lists[stop_index]
    pattern_line = pattern_lists[stop_index]

    def add_group(group_index, inner_totals):
        first_slot = group_index * group_size
        picked_dest = lax.dynamic_slice_in_dim(dest_line, first_slot, group_size)
        picked_source = lax.dynamic_slice_in_dim(source_line, first_slot, group_size)
        picked_pattern = lax.dynamic_slice_in_dim(pattern_line, first_slot, group_size)
        live_slots = (first_slot + jnp.arange(group_size, dtype=jnp.int32) < listed_count).astype(
            jnp.float32
        )
        mask_bits = unpack_bits(jnp.take(pattern_bank, picked_pattern, axis=0))
        return tile_terms(
            inner_totals,
            dest_tiles,
            source_tiles,
            picked_dest,
            picked_source,
            mask_bits,
            live_slots,
        )

    group_total = capacity // group_size
    return lax.fori_loop(0, group_total, add_group, totals)


def on_device(
    embedding,
    tile_dest,
    tile_source,
    tile_count,
    pattern_id,
    pattern_bank,
    negative_dest,
    negative_source,
):
    local_rows, feature_width = embedding.shape
    tile_size = pattern_bank.shape[2]
    cycle_size = lax.axis_size("blk")
    row_panel = lax.all_gather(embedding, "fiber", axis=0, tiled=True)
    dest_tiles = row_panel.reshape(-1, tile_size, feature_width)
    source_tiles = embedding.reshape(local_rows // tile_size, tile_size, feature_width)
    tables = (
        tile_dest[0, 0],
        tile_source[0, 0],
        tile_count[0, 0],
        pattern_id[0, 0],
        negative_dest[0, 0],
        negative_source[0, 0],
    )
    dest_zero = jnp.zeros(dest_tiles.shape, jnp.float32)
    source_zero = jnp.zeros(source_tiles.shape, jnp.float32)
    dest_sum, own_part = visit_stop(
        0, (dest_zero, source_zero), dest_tiles, source_tiles, tables, pattern_bank
    )

    def carry_stop(stop_index, carry):
        dest_sum, moving_tiles, moving_sums = carry
        moving_tiles = from_behind(moving_tiles, "blk", 1)
        moving_sums = from_behind(moving_sums, "blk", 1)
        dest_sum, moving_sums = visit_stop(
            stop_index, (dest_sum, moving_sums), dest_tiles, moving_tiles, tables, pattern_bank
        )
        return (dest_sum, moving_tiles, moving_sums)

    dest_sum, moving_tiles, moving_sums = lax.fori_loop(
        1, cycle_size, carry_stop, (dest_sum, source_tiles, own_part)
    )
    source_sum = from_behind(moving_sums, "blk", 1)
    dest_total = lax.psum_scatter(
        dest_sum.reshape(-1, feature_width), "fiber", scatter_dimension=0, tiled=True
    )
    gradient = (dest_total + source_sum.reshape(-1, feature_width)) / jnp.sqrt(
        jnp.float32(tile_size * cycle_size)
    )
    return gradient


def solution(mesh):
    in_specs = (
        P(("blk", "fiber"), None),
        P("blk", "fiber", None, None),
        P("blk", "fiber", None, None),
        P("blk", "fiber", None),
        P("blk", "fiber", None, None),
        P(),
        P("blk", "fiber", None, None),
        P("blk", "fiber", None, None),
    )
    out_specs = P(("blk", "fiber"), None)
    return jax.shard_map(
        on_device, mesh=mesh, in_specs=in_specs, out_specs=out_specs, check_vma=False
    )
```

profile of v0, /device:TPU:1, one launch (start us, length us, event | category | flops | bytes accessed | tf_op | source)
XLA Modules:
  0.0 868.2 jit_solution(11995426826140947856)
XLA Ops:
  15.0 33.5 %all-gather.2.cloned.1.call-done = bf16[4096,256]{1,0:T(8,128)(2,1)} async-done(((bf16[512,256]{1,0:T(8,128)(2,1)}), bf16[4096,256]{1,0:T(8,128)(2,1)}) %all-gather.2.cloned.1.call-update) | async-done | bytes 2097168 | tf_op jit(solution)/shard_map/all_gather | solution.py:114
  48.5 2.9 copy.32
  54.4 3.7 fusion.88
  58.0 32.2 %while.65 = (s32[]{:T(128)}, f32[32,128,256]{2,0,1:T(8,128)}, f32[4,128,256]{2,0,1:T(4,128)S(1)}, s32[24]{0:T(128)S(1)}, s32[]{:T(128)S(1)}, /*index=5*/s32[24]{...) while((s32[]{:T(128)}, f32[32,128,256]{2,0,1:T(8,128)}, ...), condition=%wide.region_1.3_spmd, body=%wide.region_0.2_spmd.sunk | while | flops 336336544 | bytes 54614732 | solution.py:98
  75.0 2.5 convolution_add_fusion.12
  85.7 2.5 convolution_add_fusion.12
  90.2 706.4 %while.67 = (s32[]{:T(128)}, f32[32,128,256]{2,0,1:T(8,128)}, bf16[4,128,256]{2,0,1:T(4,128)(2,1)}, f32[4,128,256]{2,0,1:T(4,128)S(1)}, s32[16,4]{1,0:T(8,128)S(...) while((s32[]{:T(128)}, f32[32,128,256]{2,0,1:T(8,128)}, ...), condition=%wide.region_5.0_spmd, body=%wide.region_2.6_spmd.sunk | while | flops 504829888 | bytes 107700080 | solution.py:140
  90.2 8.0 collective-permute-start
  108.3 31.1 %while.68 = (s32[]{:T(128)}, f32[32,128,256]{2,0,1:T(8,128)}, f32[4,128,256]{2,0,1:T(4,128)S(1)}, s32[24]{0:T(128)S(1)}, s32[]{:T(128)}, /*index=5*/s32[24]{0:T(...) while((s32[]{:T(128)}, f32[32,128,256]{2,0,1:T(8,128)}, ...), condition=%wide.region_4.5_spmd, body=%wide.region_3.4_spmd.sunk | while | flops 336336544 | bytes 54614732 | solution.py:98
  114.2 2.5 convolution_add_fusion.16
  134.9 2.5 convolution_add_fusion.16
  139.4 4.0 collective-permute-start
  153.4 31.1 %while.68 = (s32[]{:T(128)}, f32[32,128,256]{2,0,1:T(8,128)}, f32[4,128,256]{2,0,1:T(4,128)S(1)}, s32[24]{0:T(128)S(1)}, s32[]{:T(128)}, /*index=5*/s32[24]{0:T(...) while((s32[]{:T(128)}, f32[32,128,256]{2,0,1:T(8,128)}, ...), condition=%wide.region_4.5_spmd, body=%wide.region_3.4_spmd.sunk | while | flops 336336544 | bytes 54614732 | solution.py:98
  159.3 2.5 convolution_add_fusion.16
  180.1 2.5 convolution_add_fusion.16
  184.5 4.0 collective-permute-start
  198.6 31.1 %while.68 = (s32[]{:T(128)}, f32[32,128,256]{2,0,1:T(8,128)}, f32[4,128,256]{2,0,1:T(4,128)S(1)}, s32[24]{0:T(128)S(1)}, s32[]{:T(128)}, /*index=5*/s32[24]{0:T(...) while((s32[]{:T(128)}, f32[32,128,256]{2,0,1:T(8,128)}, ...), condition=%wide.region_4.5_spmd, body=%wide.region_3.4_spmd.sunk | while | flops 336336544 | bytes 54614732 | solution.py:98
  204.5 2.5 convolution_add_fusion.16
  214.9 2.5 convolution_add_fusion.16
  229.7 4.0 collective-permute-start
  236.5 2.8 collective-permute-done
  245.6 31.1 %while.68 = (s32[]{:T(128)}, f32[32,128,256]{2,0,1:T(8,128)}, f32[4,128,256]{2,0,1:T(4,128)S(1)}, s32[24]{0:T(128)S(1)}, s32[]{:T(128)}, /*index=5*/s32[24]{0:T(...) while((s32[]{:T(128)}, f32[32,128,256]{2,0,1:T(8,128)}, ...), condition=%wide.region_4.5_spmd, body=%wide.region_3.4_spmd.sunk | while | flops 336336544 | bytes 54614732 | solution.py:98
  251.5 2.5 convolution_add_fusion.16
  261.8 2.5 convolution_add_fusion.16
  272.2 2.5 convolution_add_fusion.16
  282.3 4.3 collective-permute-done
  292.8 31.1 %while.68 = (s32[]{:T(128)}, f32[32,128,256]{2,0,1:T(8,128)}, f32[4,128,256]{2,0,1:T(4,128)S(1)}, s32[24]{0:T(128)S(1)}, s32[]{:T(128)}, /*index=5*/s32[24]{0:T(...) while((s32[]{:T(128)}, f32[32,128,256]{2,0,1:T(8,128)}, ...), condition=%wide.region_4.5_spmd, body=%wide.region_3.4_spmd.sunk | while | flops 336336544 | bytes 54614732 | solution.py:98
  298.7 2.5 convolution_add_fusion.16
  328.3 5.5 collective-permute-done
  340.1 31.1 %while.68 = (s32[]{:T(128)}, f32[32,128,256]{2,0,1:T(8,128)}, f32[4,128,256]{2,0,1:T(4,128)S(1)}, s32[24]{0:T(128)S(1)}, s32[]{:T(128)}, /*index=5*/s32[24]{0:T(...) while((s32[]{:T(128)}, f32[32,128,256]{2,0,1:T(8,128)}, ...), condition=%wide.region_4.5_spmd, body=%wide.region_3.4_spmd.sunk | while | flops 336336544 | bytes 54614732 | solution.py:98
  346.0 2.5 convolution_add_fusion.16
  356.4 2.5 convolution_add_fusion.16
  366.7 2.5 convolution_add_fusion.16
  374.4 6.7 collective-permute-done
  387.4 31.1 %while.68 = (s32[]{:T(128)}, f32[32,128,256]{2,0,1:T(8,128)}, f32[4,128,256]{2,0,1:T(4,128)S(1)}, s32[24]{0:T(128)S(1)}, s32[]{:T(128)}, /*index=5*/s32[24]{0:T(...) while((s32[]{:T(128)}, f32[32,128,256]{2,0,1:T(8,128)}, ...), condition=%wide.region_4.5_spmd, body=%wide.region_3.4_spmd.sunk | while | flops 336336544 | bytes 54614732 | solution.py:98
  393.3 2.5 convolution_add_fusion.16
  414.0 2.5 convolution_add_fusion.16
  421.3 7.1 collective-permute-done
  434.6 31.1 %while.68 = (s32[]{:T(128)}, f32[32,128,256]{2,0,1:T(8,128)}, f32[4,128,256]{2,0,1:T(4,128)S(1)}, s32[24]{0:T(128)S(1)}, s32[]{:T(128)}, /*index=5*/s32[24]{0:T(...) while((s32[]{:T(128)}, f32[32,128,256]{2,0,1:T(8,128)}, ...), condition=%wide.region_4.5_spmd, body=%wide.region_3.4_spmd.sunk | while | flops 336336544 | bytes 54614732 | solution.py:98
  440.5 2.5 convolution_add_fusion.16
  468.5 7.1 collective-permute-done
  481.9 31.1 %while.68 = (s32[]{:T(128)}, f32[32,128,256]{2,0,1:T(8,128)}, f32[4,128,256]{2,0,1:T(4,128)S(1)}, s32[24]{0:T(128)S(1)}, s32[]{:T(128)}, /*index=5*/s32[24]{0:T(...) while((s32[]{:T(128)}, f32[32,128,256]{2,0,1:T(8,128)}, ...), condition=%wide.region_4.5_spmd, body=%wide.region_3.4_spmd.sunk | while | flops 336336544 | bytes 54614732 | solution.py:98
  487.8 2.5 convolution_add_fusion.16
  515.8 7.1 collective-permute-done
  529.2 31.1 %while.68 = (s32[]{:T(128)}, f32[32,128,256]{2,0,1:T(8,128)}, f32[4,128,256]{2,0,1:T(4,128)S(1)}, s32[24]{0:T(128)S(1)}, s32[]{:T(128)}, /*index=5*/s32[24]{0:T(...) while((s32[]{:T(128)}, f32[32,128,256]{2,0,1:T(8,128)}, ...), condition=%wide.region_4.5_spmd, body=%wide.region_3.4_spmd.sunk | while | flops 336336544 | bytes 54614732 | solution.py:98
  535.1 2.5 convolution_add_fusion.16
  563.1 7.1 collective-permute-done
  576.4 31.1 %while.68 = (s32[]{:T(128)}, f32[32,128,256]{2,0,1:T(8,128)}, f32[4,128,256]{2,0,1:T(4,128)S(1)}, s32[24]{0:T(128)S(1)}, s32[]{:T(128)}, /*index=5*/s32[24]{0:T(...) while((s32[]{:T(128)}, f32[32,128,256]{2,0,1:T(8,128)}, ...), condition=%wide.region_4.5_spmd, body=%wide.region_3.4_spmd.sunk | while | flops 336336544 | bytes 54614732 | solution.py:98
  582.3 2.5 convolution_add_fusion.16
  610.3 7.1 collective-permute-done
  623.7 31.1 %while.68 = (s32[]{:T(128)}, f32[32,128,256]{2,0,1:T(8,128)}, f32[4,128,256]{2,0,1:T(4,128)S(1)}, s32[24]{0:T(128)S(1)}, s32[]{:T(128)}, /*index=5*/s32[24]{0:T(...) while((s32[]{:T(128)}, f32[32,128,256]{2,0,1:T(8,128)}, ...), condition=%wide.region_4.5_spmd, body=%wide.region_3.4_spmd.sunk | while | flops 336336544 | bytes 54614732 | solution.py:98
  629.6 2.5 convolution_add_fusion.16
  657.6 7.1 collective-permute-done
  671.0 31.1 %while.68 = (s32[]{:T(128)}, f32[32,128,256]{2,0,1:T(8,128)}, f32[4,128,256]{2,0,1:T(4,128)S(1)}, s32[24]{0:T(128)S(1)}, s32[]{:T(128)}, /*index=5*/s32[24]{0:T(...) while((s32[]{:T(128)}, f32[32,128,256]{2,0,1:T(8,128)}, ...), condition=%wide.region_4.5_spmd, body=%wide.region_3.4_spmd.sunk | while | flops 336336544 | bytes 54614732 | solution.py:98
  676.9 2.5 convolution_add_fusion.16
  704.9 7.1 collective-permute-done
  718.2 31.1 %while.68 = (s32[]{:T(128)}, f32[32,128,256]{2,0,1:T(8,128)}, f32[4,128,256]{2,0,1:T(4,128)S(1)}, s32[24]{0:T(128)S(1)}, s32[]{:T(128)}, /*index=5*/s32[24]{0:T(...) while((s32[]{:T(128)}, f32[32,128,256]{2,0,1:T(8,128)}, ...), condition=%wide.region_4.5_spmd, body=%wide.region_3.4_spmd.sunk | while | flops 336336544 | bytes 54614732 | solution.py:98
  724.1 2.5 convolution_add_fusion.16
  752.1 7.1 collective-permute-done
  765.5 31.1 %while.68 = (s32[]{:T(128)}, f32[32,128,256]{2,0,1:T(8,128)}, f32[4,128,256]{2,0,1:T(4,128)S(1)}, s32[24]{0:T(128)S(1)}, s32[]{:T(128)}, /*index=5*/s32[24]{0:T(...) while((s32[]{:T(128)}, f32[32,128,256]{2,0,1:T(8,128)}, ...), condition=%wide.region_4.5_spmd, body=%wide.region_3.4_spmd.sunk | while | flops 336336544 | bytes 54614732 | solution.py:98
  771.4 2.5 convolution_add_fusion.16
  796.6 6.6 copy.41
  803.3 9.7 %collective-permute-done.2 = f32[4,128,256]{2,0,1:T(4,128)S(1)} collective-permute-done((f32[4,128,256]{2,0,1:T(4,128)S(1)}, f32[4,128,256]{2,0,1:T(4,128)S(1)}, u32[]{:S(2)}, u32[]{:S(2)}) %collective-permute-start.2) | collective-permute-done | bytes 524320 | tf_op jit(solution)/shard_map/ppermute | solution.py:11
  813.1 46.3 %reduce-scatter.2.cloned.1.call-done = f32[512,256]{1,0:T(8,128)} async-done(((f32[4096,256]{1,0:T(8,128)}), f32[512,256]{1,0:T(8,128)}) %reduce-scatter.2.cloned.1.call-update) | async-done | bytes 524304 | tf_op jit(solution)/shard_map/reduce_scatter | solution.py:144
  (1243 shorter events, 588.7 us)
Async XLA Ops:
  6.5 42.0 %all-gather.2.cloned.1.call-start = ((), (), s32[]{:S(2)}) async-start(), calls=%async_computation.1 | async-start | bytes 2359296 | tf_op jit(solution)/shard_map/all_gather | solution.py:114
  7.3 852.2 %reduce-scatter.2.cloned.1.call-start = ((), (), s32[]{:S(2)}) async-start(), calls=%async_computation.2 | async-start | bytes 4718592 | tf_op jit(solution)/shard_map/reduce_scatter | solution.py:144
  48.5 2.9 copy-start.6
  53.0 5.1 copy-start.7
  72.5 2.4 copy-start
  90.2 11.7 %collective-permute-start = (bf16[4,128,256]{2,0,1:T(4,128)(2,1)}, bf16[4,128,256]{2,0,1:T(4,128)(2,1)S(1)}, u32[]{:S(2)}, u32[]{:S(2)}) collective-permute-start(bf16[4,128,256]{2,0,1:T(4,128)(2,1)} %get-tuple-element.1137), channel_id=1, source_target_pairs={{0,8},{8,16},{16,24},{24,32},{32,40},{40,48},{48,56},{56,64},{64,7... | collective-permute-start | bytes 786440 | tf_op jit(solution)/shard_map/while/body/eval_jaxpr/ppermute | solution.py:11
  98.2 9.1 %collective-permute-start.1 = (f32[4,128,256]{2,0,1:T(4,128)S(1)}, f32[4,128,256]{2,0,1:T(4,128)S(1)}, u32[]{:S(2)}, u32[]{:S(2)}) collective-permute-start(f32[4,128,256]{2,0,1:T(4,128)S(1)} %get-tuple-element.1138), channel_id=1, source_target_pairs={{0,8},{8,16},{16,24},{24,32},{32,40},{40,48},{48,56},{56,64},{64,7... | collective-permute-start | bytes 1572872 | tf_op jit(solution)/shard_map/while/body/eval_jaxpr/ppermute | solution.py:11
  98.2 5.4 copy-start.2
  111.8 2.4 copy-start.4
  139.4 7.6 collective-permute-start
  143.4 9.1 %collective-permute-start.1 = (f32[4,128,256]{2,0,1:T(4,128)S(1)}, f32[4,128,256]{2,0,1:T(4,128)S(1)}, u32[]{:S(2)}, u32[]{:S(2)}) collective-permute-start(f32[4,128,256]{2,0,1:T(4,128)S(1)} %get-tuple-element.1138), channel_id=1, source_target_pairs={{0,8},{8,16},{16,24},{24,32},{32,40},{40,48},{48,56},{56,64},{64,7... | collective-permute-start | bytes 1572872 | tf_op jit(solution)/shard_map/while/body/eval_jaxpr/ppermute | solution.py:11
  143.4 5.4 copy-start.2
  184.5 7.6 collective-permute-start
  188.5 9.1 %collective-permute-start.1 = (f32[4,128,256]{2,0,1:T(4,128)S(1)}, f32[4,128,256]{2,0,1:T(4,128)S(1)}, u32[]{:S(2)}, u32[]{:S(2)}) collective-permute-start(f32[4,128,256]{2,0,1:T(4,128)S(1)} %get-tuple-element.1138), channel_id=1, source_target_pairs={{0,8},{8,16},{16,24},{24,32},{32,40},{40,48},{48,56},{56,64},{64,7... | collective-permute-start | bytes 1572872 | tf_op jit(solution)/shard_map/while/body/eval_jaxpr/ppermute | solution.py:11
  188.6 5.4 copy-start.2
  229.7 9.6 %collective-permute-start = (bf16[4,128,256]{2,0,1:T(4,128)(2,1)}, bf16[4,128,256]{2,0,1:T(4,128)(2,1)S(1)}, u32[]{:S(2)}, u32[]{:S(2)}) collective-permute-start(bf16[4,128,256]{2,0,1:T(4,128)(2,1)} %get-tuple-element.1137), channel_id=1, source_target_pairs={{0,8},{8,16},{16,24},{24,32},{32,40},{40,48},{48,56},{56,64},{64,7... | collective-permute-start | bytes 786440 | tf_op jit(solution)/shard_map/while/body/eval_jaxpr/ppermute | solution.py:11
  233.7 9.9 %collective-permute-start.1 = (f32[4,128,256]{2,0,1:T(4,128)S(1)}, f32[4,128,256]{2,0,1:T(4,128)S(1)}, u32[]{:S(2)}, u32[]{:S(2)}) collective-permute-start(f32[4,128,256]{2,0,1:T(4,128)S(1)} %get-tuple-element.1138), channel_id=1, source_target_pairs={{0,8},{8,16},{16,24},{24,32},{32,40},{40,48},{48,56},{56,64},{64,7... | collective-permute-start | bytes 1572872 | tf_op jit(solution)/shard_map/while/body/eval_jaxpr/ppermute | solution.py:11
  233.7 7.4 copy-start.2
  249.0 2.4 copy-start.4
  276.6 9.9 %collective-permute-start = (bf16[4,128,256]{2,0,1:T(4,128)(2,1)}, bf16[4,128,256]{2,0,1:T(4,128)(2,1)S(1)}, u32[]{:S(2)}, u32[]{:S(2)}) collective-permute-start(bf16[4,128,256]{2,0,1:T(4,128)(2,1)} %get-tuple-element.1137), channel_id=1, source_target_pairs={{0,8},{8,16},{16,24},{24,32},{32,40},{40,48},{48,56},{56,64},{64,7... | collective-permute-start | bytes 786440 | tf_op jit(solution)/shard_map/while/body/eval_jaxpr/ppermute | solution.py:11
  278.9 12.0 %collective-permute-start.1 = (f32[4,128,256]{2,0,1:T(4,128)S(1)}, f32[4,128,256]{2,0,1:T(4,128)S(1)}, u32[]{:S(2)}, u32[]{:S(2)}) collective-permute-start(f32[4,128,256]{2,0,1:T(4,128)S(1)} %get-tuple-element.1138), channel_id=1, source_target_pairs={{0,8},{8,16},{16,24},{24,32},{32,40},{40,48},{48,56},{56,64},{64,7... | collective-permute-start | bytes 1572872 | tf_op jit(solution)/shard_map/while/body/eval_jaxpr/ppermute | solution.py:11
  279.5 8.9 %copy-start.2 = (f32[32,128,256]{2,0,1:T(8,128)S(1)}, f32[32,128,256]{2,0,1:T(8,128)}, u32[]{:S(2)}) copy-start(f32[32,128,256]{2,0,1:T(8,128)} %get-tuple-element.1136) | copy-start | bytes 12582916 | tf_op jit(solution)/shard_map/while
  296.3 2.4 copy-start.4
  323.9 9.9 %collective-permute-start = (bf16[4,128,256]{2,0,1:T(4,128)(2,1)}, bf16[4,128,256]{2,0,1:T(4,128)(2,1)S(1)}, u32[]{:S(2)}, u32[]{:S(2)}) collective-permute-start(bf16[4,128,256]{2,0,1:T(4,128)(2,1)} %get-tuple-element.1137), channel_id=1, source_target_pairs={{0,8},{8,16},{16,24},{24,32},{32,40},{40,48},{48,56},{56,64},{64,7... | collective-permute-start | bytes 786440 | tf_op jit(solution)/shard_map/while/body/eval_jaxpr/ppermute | solution.py:11
  324.5 13.6 %collective-permute-start.1 = (f32[4,128,256]{2,0,1:T(4,128)S(1)}, f32[4,128,256]{2,0,1:T(4,128)S(1)}, u32[]{:S(2)}, u32[]{:S(2)}) collective-permute-start(f32[4,128,256]{2,0,1:T(4,128)S(1)} %get-tuple-element.1138), channel_id=1, source_target_pairs={{0,8},{8,16},{16,24},{24,32},{32,40},{40,48},{48,56},{56,64},{64,7... | collective-permute-start | bytes 1572872 | tf_op jit(solution)/shard_map/while/body/eval_jaxpr/ppermute | solution.py:11
  325.5 10.1 %copy-start.2 = (f32[32,128,256]{2,0,1:T(8,128)S(1)}, f32[32,128,256]{2,0,1:T(8,128)}, u32[]{:S(2)}) copy-start(f32[32,128,256]{2,0,1:T(8,128)} %get-tuple-element.1136) | copy-start | bytes 12582916 | tf_op jit(solution)/shard_map/while
  343.5 2.4 copy-start.4
  371.2 9.9 %collective-permute-start = (bf16[4,128,256]{2,0,1:T(4,128)(2,1)}, bf16[4,128,256]{2,0,1:T(4,128)(2,1)S(1)}, u32[]{:S(2)}, u32[]{:S(2)}) collective-permute-start(bf16[4,128,256]{2,0,1:T(4,128)(2,1)} %get-tuple-element.1137), channel_id=1, source_target_pairs={{0,8},{8,16},{16,24},{24,32},{32,40},{40,48},{48,56},{56,64},{64,7... | collective-permute-start | bytes 786440 | tf_op jit(solution)/shard_map/while/body/eval_jaxpr/ppermute | solution.py:11
  371.2 14.2 %collective-permute-start.1 = (f32[4,128,256]{2,0,1:T(4,128)S(1)}, f32[4,128,256]{2,0,1:T(4,128)S(1)}, u32[]{:S(2)}, u32[]{:S(2)}) collective-permute-start(f32[4,128,256]{2,0,1:T(4,128)S(1)} %get-tuple-element.1138), channel_id=1, source_target_pairs={{0,8},{8,16},{16,24},{24,32},{32,40},{40,48},{48,56},{56,64},{64,7... | collective-permute-start | bytes 1572872 | tf_op jit(solution)/shard_map/while/body/eval_jaxpr/ppermute | solution.py:11
  371.6 11.3 %copy-start.2 = (f32[32,128,256]{2,0,1:T(8,128)S(1)}, f32[32,128,256]{2,0,1:T(8,128)}, u32[]{:S(2)}) copy-start(f32[32,128,256]{2,0,1:T(8,128)} %get-tuple-element.1136) | copy-start | bytes 12582916 | tf_op jit(solution)/shard_map/while
  390.8 2.4 copy-start.4
  418.4 9.9 %collective-permute-start = (bf16[4,128,256]{2,0,1:T(4,128)(2,1)}, bf16[4,128,256]{2,0,1:T(4,128)(2,1)S(1)}, u32[]{:S(2)}, u32[]{:S(2)}) collective-permute-start(bf16[4,128,256]{2,0,1:T(4,128)(2,1)} %get-tuple-element.1137), channel_id=1, source_target_pairs={{0,8},{8,16},{16,24},{24,32},{32,40},{40,48},{48,56},{56,64},{64,7... | collective-permute-start | bytes 786440 | tf_op jit(solution)/shard_map/while/body/eval_jaxpr/ppermute | solution.py:11
  418.4 14.2 %collective-permute-start.1 = (f32[4,128,256]{2,0,1:T(4,128)S(1)}, f32[4,128,256]{2,0,1:T(4,128)S(1)}, u32[]{:S(2)}, u32[]{:S(2)}) collective-permute-start(f32[4,128,256]{2,0,1:T(4,128)S(1)} %get-tuple-element.1138), channel_id=1, source_target_pairs={{0,8},{8,16},{16,24},{24,32},{32,40},{40,48},{48,56},{56,64},{64,7... | collective-permute-start | bytes 1572872 | tf_op jit(solution)/shard_map/while/body/eval_jaxpr/ppermute | solution.py:11
  418.5 11.7 %copy-start.2 = (f32[32,128,256]{2,0,1:T(8,128)S(1)}, f32[32,128,256]{2,0,1:T(8,128)}, u32[]{:S(2)}) copy-start(f32[32,128,256]{2,0,1:T(8,128)} %get-tuple-element.1136) | copy-start | bytes 12582916 | tf_op jit(solution)/shard_map/while
  438.1 2.4 copy-start.4
  465.7 9.9 %collective-permute-start = (bf16[4,128,256]{2,0,1:T(4,128)(2,1)}, bf16[4,128,256]{2,0,1:T(4,128)(2,1)S(1)}, u32[]{:S(2)}, u32[]{:S(2)}) collective-permute-start(bf16[4,128,256]{2,0,1:T(4,128)(2,1)} %get-tuple-element.1137), channel_id=1, source_target_pairs={{0,8},{8,16},{16,24},{24,32},{32,40},{40,48},{48,56},{56,64},{64,7... | collective-permute-start | bytes 786440 | tf_op jit(solution)/shard_map/while/body/eval_jaxpr/ppermute | solution.py:11
  465.7 14.2 %collective-permute-start.1 = (f32[4,128,256]{2,0,1:T(4,128)S(1)}, f32[4,128,256]{2,0,1:T(4,128)S(1)}, u32[]{:S(2)}, u32[]{:S(2)}) collective-permute-start(f32[4,128,256]{2,0,1:T(4,128)S(1)} %get-tuple-element.1138), channel_id=1, source_target_pairs={{0,8},{8,16},{16,24},{24,32},{32,40},{40,48},{48,56},{56,64},{64,7... | collective-permute-start | bytes 1572872 | tf_op jit(solution)/shard_map/while/body/eval_jaxpr/ppermute | solution.py:11
  465.7 11.7 %copy-start.2 = (f32[32,128,256]{2,0,1:T(8,128)S(1)}, f32[32,128,256]{2,0,1:T(8,128)}, u32[]{:S(2)}) copy-start(f32[32,128,256]{2,0,1:T(8,128)} %get-tuple-element.1136) | copy-start | bytes 12582916 | tf_op jit(solution)/shard_map/while
  485.3 2.4 copy-start.4
  513.0 9.9 %collective-permute-start = (bf16[4,128,256]{2,0,1:T(4,128)(2,1)}, bf16[4,128,256]{2,0,1:T(4,128)(2,1)S(1)}, u32[]{:S(2)}, u32[]{:S(2)}) collective-permute-start(bf16[4,128,256]{2,0,1:T(4,128)(2,1)} %get-tuple-element.1137), channel_id=1, source_target_pairs={{0,8},{8,16},{16,24},{24,32},{32,40},{40,48},{48,56},{56,64},{64,7... | collective-permute-start | bytes 786440 | tf_op jit(solution)/shard_map/while/body/eval_jaxpr/ppermute | solution.py:11
  513.0 14.2 %collective-permute-start.1 = (f32[4,128,256]{2,0,1:T(4,128)S(1)}, f32[4,128,256]{2,0,1:T(4,128)S(1)}, u32[]{:S(2)}, u32[]{:S(2)}) collective-permute-start(f32[4,128,256]{2,0,1:T(4,128)S(1)} %get-tuple-element.1138), channel_id=1, source_target_pairs={{0,8},{8,16},{16,24},{24,32},{32,40},{40,48},{48,56},{56,64},{64,7... | collective-permute-start | bytes 1572872 | tf_op jit(solution)/shard_map/while/body/eval_jaxpr/ppermute | solution.py:11
  513.0 11.7 %copy-start.2 = (f32[32,128,256]{2,0,1:T(8,128)S(1)}, f32[32,128,256]{2,0,1:T(8,128)}, u32[]{:S(2)}) copy-start(f32[32,128,256]{2,0,1:T(8,128)} %get-tuple-element.1136) | copy-start | bytes 12582916 | tf_op jit(solution)/shard_map/while
  532.6 2.4 copy-start.4
  560.2 9.9 %collective-permute-start = (bf16[4,128,256]{2,0,1:T(4,128)(2,1)}, bf16[4,128,256]{2,0,1:T(4,128)(2,1)S(1)}, u32[]{:S(2)}, u32[]{:S(2)}) collective-permute-start(bf16[4,128,256]{2,0,1:T(4,128)(2,1)} %get-tuple-element.1137), channel_id=1, source_target_pairs={{0,8},{8,16},{16,24},{24,32},{32,40},{40,48},{48,56},{56,64},{64,7... | collective-permute-start | bytes 786440 | tf_op jit(solution)/shard_map/while/body/eval_jaxpr/ppermute | solution.py:11
  560.2 14.2 %collective-permute-start.1 = (f32[4,128,256]{2,0,1:T(4,128)S(1)}, f32[4,128,256]{2,0,1:T(4,128)S(1)}, u32[]{:S(2)}, u32[]{:S(2)}) collective-permute-start(f32[4,128,256]{2,0,1:T(4,128)S(1)} %get-tuple-element.1138), channel_id=1, source_target_pairs={{0,8},{8,16},{16,24},{24,32},{32,40},{40,48},{48,56},{56,64},{64,7... | collective-permute-start | bytes 1572872 | tf_op jit(solution)/shard_map/while/body/eval_jaxpr/ppermute | solution.py:11
  560.3 11.7 %copy-start.2 = (f32[32,128,256]{2,0,1:T(8,128)S(1)}, f32[32,128,256]{2,0,1:T(8,128)}, u32[]{:S(2)}) copy-start(f32[32,128,256]{2,0,1:T(8,128)} %get-tuple-element.1136) | copy-start | bytes 12582916 | tf_op jit(solution)/shard_map/while
  579.9 2.4 copy-start.4
  607.5 9.9 %collective-permute-start = (bf16[4,128,256]{2,0,1:T(4,128)(2,1)}, bf16[4,128,256]{2,0,1:T(4,128)(2,1)S(1)}, u32[]{:S(2)}, u32[]{:S(2)}) collective-permute-start(bf16[4,128,256]{2,0,1:T(4,128)(2,1)} %get-tuple-element.1137), channel_id=1, source_target_pairs={{0,8},{8,16},{16,24},{24,32},{32,40},{40,48},{48,56},{56,64},{64,7... | collective-permute-start | bytes 786440 | tf_op jit(solution)/shard_map/while/body/eval_jaxpr/ppermute | solution.py:11
  607.5 14.2 %collective-permute-start.1 = (f32[4,128,256]{2,0,1:T(4,128)S(1)}, f32[4,128,256]{2,0,1:T(4,128)S(1)}, u32[]{:S(2)}, u32[]{:S(2)}) collective-permute-start(f32[4,128,256]{2,0,1:T(4,128)S(1)} %get-tuple-element.1138), channel_id=1, source_target_pairs={{0,8},{8,16},{16,24},{24,32},{32,40},{40,48},{48,56},{56,64},{64,7... | collective-permute-start | bytes 1572872 | tf_op jit(solution)/shard_map/while/body/eval_jaxpr/ppermute | solution.py:11
  607.5 11.7 %copy-start.2 = (f32[32,128,256]{2,0,1:T(8,128)S(1)}, f32[32,128,256]{2,0,1:T(8,128)}, u32[]{:S(2)}) copy-start(f32[32,128,256]{2,0,1:T(8,128)} %get-tuple-element.1136) | copy-start | bytes 12582916 | tf_op jit(solution)/shard_map/while
  627.2 2.4 copy-start.4
  654.8 9.9 %collective-permute-start = (bf16[4,128,256]{2,0,1:T(4,128)(2,1)}, bf16[4,128,256]{2,0,1:T(4,128)(2,1)S(1)}, u32[]{:S(2)}, u32[]{:S(2)}) collective-permute-start(bf16[4,128,256]{2,0,1:T(4,128)(2,1)} %get-tuple-element.1137), channel_id=1, source_target_pairs={{0,8},{8,16},{16,24},{24,32},{32,40},{40,48},{48,56},{56,64},{64,7... | collective-permute-start | bytes 786440 | tf_op jit(solution)/shard_map/while/body/eval_jaxpr/ppermute | solution.py:11
  654.8 14.2 %collective-permute-start.1 = (f32[4,128,256]{2,0,1:T(4,128)S(1)}, f32[4,128,256]{2,0,1:T(4,128)S(1)}, u32[]{:S(2)}, u32[]{:S(2)}) collective-permute-start(f32[4,128,256]{2,0,1:T(4,128)S(1)} %get-tuple-element.1138), channel_id=1, source_target_pairs={{0,8},{8,16},{16,24},{24,32},{32,40},{40,48},{48,56},{56,64},{64,7... | collective-permute-start | bytes 1572872 | tf_op jit(solution)/shard_map/while/body/eval_jaxpr/ppermute | solution.py:11
  654.8 11.7 %copy-start.2 = (f32[32,128,256]{2,0,1:T(8,128)S(1)}, f32[32,128,256]{2,0,1:T(8,128)}, u32[]{:S(2)}) copy-start(f32[32,128,256]{2,0,1:T(8,128)} %get-tuple-element.1136) | copy-start | bytes 12582916 | tf_op jit(solution)/shard_map/while
  674.4 2.4 copy-start.4
  702.0 9.9 %collective-permute-start = (bf16[4,128,256]{2,0,1:T(4,128)(2,1)}, bf16[4,128,256]{2,0,1:T(4,128)(2,1)S(1)}, u32[]{:S(2)}, u32[]{:S(2)}) collective-permute-start(bf16[4,128,256]{2,0,1:T(4,128)(2,1)} %get-tuple-element.1137), channel_id=1, source_target_pairs={{0,8},{8,16},{16,24},{24,32},{32,40},{40,48},{48,56},{56,64},{64,7... | collective-permute-start | bytes 786440 | tf_op jit(solution)/shard_map/while/body/eval_jaxpr/ppermute | solution.py:11
  702.1 14.2 %collective-permute-start.1 = (f32[4,128,256]{2,0,1:T(4,128)S(1)}, f32[4,128,256]{2,0,1:T(4,128)S(1)}, u32[]{:S(2)}, u32[]{:S(2)}) collective-permute-start(f32[4,128,256]{2,0,1:T(4,128)S(1)} %get-tuple-element.1138), channel_id=1, source_target_pairs={{0,8},{8,16},{16,24},{24,32},{32,40},{40,48},{48,56},{56,64},{64,7... | collective-permute-start | bytes 1572872 | tf_op jit(solution)/shard_map/while/body/eval_jaxpr/ppermute | solution.py:11
  702.1 11.7 %copy-start.2 = (f32[32,128,256]{2,0,1:T(8,128)S(1)}, f32[32,128,256]{2,0,1:T(8,128)}, u32[]{:S(2)}) copy-start(f32[32,128,256]{2,0,1:T(8,128)} %get-tuple-element.1136) | copy-start | bytes 12582916 | tf_op jit(solution)/shard_map/while
  721.7 2.4 copy-start.4
  749.3 9.9 %collective-permute-start = (bf16[4,128,256]{2,0,1:T(4,128)(2,1)}, bf16[4,128,256]{2,0,1:T(4,128)(2,1)S(1)}, u32[]{:S(2)}, u32[]{:S(2)}) collective-permute-start(bf16[4,128,256]{2,0,1:T(4,128)(2,1)} %get-tuple-element.1137), channel_id=1, source_target_pairs={{0,8},{8,16},{16,24},{24,32},{32,40},{40,48},{48,56},{56,64},{64,7... | collective-permute-start | bytes 786440 | tf_op jit(solution)/shard_map/while/body/eval_jaxpr/ppermute | solution.py:11
  749.3 14.2 %collective-permute-start.1 = (f32[4,128,256]{2,0,1:T(4,128)S(1)}, f32[4,128,256]{2,0,1:T(4,128)S(1)}, u32[]{:S(2)}, u32[]{:S(2)}) collective-permute-start(f32[4,128,256]{2,0,1:T(4,128)S(1)} %get-tuple-element.1138), channel_id=1, source_target_pairs={{0,8},{8,16},{16,24},{24,32},{32,40},{40,48},{48,56},{56,64},{64,7... | collective-permute-start | bytes 1572872 | tf_op jit(solution)/shard_map/while/body/eval_jaxpr/ppermute | solution.py:11
  749.3 11.7 %copy-start.2 = (f32[32,128,256]{2,0,1:T(8,128)S(1)}, f32[32,128,256]{2,0,1:T(8,128)}, u32[]{:S(2)}) copy-start(f32[32,128,256]{2,0,1:T(8,128)} %get-tuple-element.1136) | copy-start | bytes 12582916 | tf_op jit(solution)/shard_map/while
  769.0 2.4 copy-start.4
  803.2 9.8 %collective-permute-start.2 = (f32[4,128,256]{2,0,1:T(4,128)S(1)}, f32[4,128,256]{2,0,1:T(4,128)S(1)}, u32[]{:S(2)}, u32[]{:S(2)}) collective-permute-start(f32[4,128,256]{2,0,1:T(4,128)S(1)} %get-tuple-element.681), channel_id=1, source_target_pairs={{0,8},{8,16},{16,24},{24,32},{32,40},{40,48},{48,56},{56,64},{64,7... | collective-permute-start | bytes 1572872 | tf_op jit(solution)/shard_map/ppermute | solution.py:11
  (97 other events, 207.2 us)
Sparse Core Ops, SparseCore 0:
  9.0 39.4 all-gather.1
  803.3 56.1 reduce-scatter.1
where the time goes:
time: 870 us; the launch traced here: 868 us
  matrix products  357 us (41%)
  local copies, waits for them, and re-layouts  251 us (29%)
  waiting for transfers between devices  173 us (20%)
  other arithmetic  44.2 us (5%)
  starting transfers between devices  25.2 us (3%)
  between operations  13.5 us (2%)
    dot_general x64, matrix products, tile_terms(): jnp.einsum('gp,gid->pid', dest_pick.astype(jnp.float32), to_dest, precisi...  160 us
    while x267, local copies, waits for them, and re-layouts  117 us
    ppermute x31, waiting for transfers between devices, from_behind(): lax.ppermute(shard, axis, [(i, (i + by) % devices) for i in range(devices)])  92 us
    dot_general x64, matrix products, tile_terms(): jnp.einsum('gp,gjd->pjd', source_pick.astype(jnp.float32), to_source, pre...  82.7 us
    gather x48, local copies, waits for them, and re-layouts, add_group(): mask_bits = unpack_bits(jnp.take(pattern_bank, picked_pattern, axis=0))  71 us
    reduce_scatter x1, waiting for transfers between devices, on_device(): lax.psum_scatter(dest_sum.reshape(-1, feature_width), 'fiber', scatter_di...  46.3 us
    all_gather x1, waiting for transfers between devices, on_device(): row_panel = lax.all_gather(embedding, 'fiber', axis=0, tiled=True)  33.5 us
    and x48, other arithmetic, add_group(): mask_bits = unpack_bits(jnp.take(pattern_bank, picked_pattern, axis=0))  32.2 us
  transfers between devices with their start and end apart: 33, of which 21 were waited for; matrix products, arithmetic and copies ran while one was open for 13% of the time, Pallas kernels for 0%

commit v1 on v0

v1 whole, which is shorter than its diff:
```python
import functools
import math

import jax
import jax.numpy as jnp
from jax import lax
from jax.experimental import pallas as pl
from jax.experimental.pallas import tpu as pltpu
from jax.sharding import PartitionSpec as P

ZS, XS, YS = 4, 2, 4
T = 128
MESH = pl.DeviceIdType.MESH
UNROLL = 4
DEST_BITS, BANK_BITS = 6, 7


def place():
    b, f = lax.axis_index("blk"), lax.axis_index("fiber")
    return b // 4, (b // 2) % 2, b % 2, f // YS, f % YS


def blk_of(z, xh, c):
    return ((z % ZS) * XS + xh) * 2 + c


def fiber_of(xl, y):
    return xl * YS + y % YS


def peers():
    z, xh, c, xl, y = place()
    b, f = blk_of(z, xh, c), fiber_of(xl, y)
    return {
        "sib": (blk_of(z, xh, 1 - c), f),
        "xh": (blk_of(z, 1 - xh, c), f),
        "z+": (blk_of(z + 1, xh, c), f),
        "z-": (blk_of(z + 3, xh, c), f),
        "xl": (b, fiber_of(1 - xl, y)),
        "y+": (b, fiber_of(xl, y + 1)),
        "y-": (b, fiber_of(xl, y + 3)),
    }


def meet(to):
    barrier = pltpu.get_barrier_semaphore()
    for device in to.values():
        pl.semaphore_signal(barrier, inc=1, device_id=device, device_id_type=MESH)
    pl.semaphore_wait(barrier, len(to))


def gather_kernel(e_ref, d_ref, g_ref, send, recv, local):
    rows = e_ref.shape[0]
    z, xh, c, xl, y = place()
    to = peers()

    def g_at(zz, xx, cc):
        return g_ref.at[pl.ds(blk_of(zz, xx, cc) * rows, rows)]

    def d_at(xx, yy):
        return d_ref.at[pl.ds(fiber_of(xx, yy) * rows, rows)]

    copies = {}

    def push(name, src, dst, peer):
        k = len(copies)
        copies[name] = pltpu.make_async_remote_copy(
            src_ref=src,
            dst_ref=dst,
            send_sem=send.at[k],
            recv_sem=recv.at[k],
            device_id=to[peer],
            device_id_type=MESH,
        )
        copies[name].start()

    def got(name):
        copies[name].wait_recv()

    def share(name, zz, xx):
        push(name, g_at(zz, xx, c), g_at(zz, xx, c), "sib")

    meet(to)
    own_g, own_d = g_at(z, xh, c), d_at(xl, y)
    push("z+", e_ref, own_g, "z+")
    push("y+", e_ref, own_d, "y+")
    push("z-", e_ref, own_g, "z-")
    push("y-", e_ref, own_d, "y-")
    push("xl", e_ref, own_d, "xl")
    push("xh", e_ref, own_g, "xh")
    push("s0", e_ref, own_g, "sib")
    keep_d = pltpu.make_async_copy(e_ref, own_d, local.at[0])
    keep_g = pltpu.make_async_copy(e_ref, own_g, local.at[1])
    keep_d.start()
    keep_g.start()
    got("xl")
    push("xl+", d_at(1 - xl, y), d_at(1 - xl, y), "y+")
    push("xl-", d_at(1 - xl, y), d_at(1 - xl, y), "y-")
    got("z+")
    push("z++", g_at(z + 3, xh, c), g_at(z + 3, xh, c), "z+")
    share("s1", z + 3, xh)
    got("y+")
    push("y++", d_at(xl, y + 3), d_at(xl, y + 3), "y+")
    got("xh")
    push("xh+", g_at(z, 1 - xh, c), g_at(z, 1 - xh, c), "z+")
    push("xh-", g_at(z, 1 - xh, c), g_at(z, 1 - xh, c), "z-")
    share("s2", z, 1 - xh)
    got("z-")
    share("s3", z + 1, xh)
    got("y-")
    got("xl-")
    push("xl--", d_at(1 - xl, y + 1), d_at(1 - xl, y + 1), "y-")
    got("xh-")
    push("xh--", g_at(z + 1, 1 - xh, c), g_at(z + 1, 1 - xh, c), "z-")
    share("s4", z + 1, 1 - xh)
    got("z++")
    share("s5", z + 2, xh)
    got("xh+")
    share("s6", z + 3, 1 - xh)
    got("xh--")
    share("s7", z + 2, 1 - xh)
    for name in ("xl+", "y++", "xl--", "s0", "s1", "s2", "s3", "s4", "s5", "s6", "s7"):
        got(name)
    for copy in copies.values():
        copy.wait_send()
    keep_d.wait()
    keep_g.wait()


def gather(e):
    rows, width = e.shape
    return pl.pallas_call(
        gather_kernel,
        out_shape=(
            jax.ShapeDtypeStruct((XS * YS * rows, width), e.dtype),
            jax.ShapeDtypeStruct((ZS * XS * 2 * rows, width), e.dtype),
        ),
        in_specs=[pl.BlockSpec(memory_space=pl.ANY)],
        out_specs=(pl.BlockSpec(memory_space=pl.ANY),) * 2,
        scratch_shapes=[
            pltpu.SemaphoreType.DMA((22,)),
            pltpu.SemaphoreType.DMA((22,)),
            pltpu.SemaphoreType.DMA((2,)),
        ],
        compiler_params=pltpu.CompilerParams(collective_id=0, has_side_effects=True),
    )(e)


def pair_lists(dest, source, count, pattern, neg_dest, neg_source, bank_size, dest_tiles, sub):
    stops, cap = dest.shape
    neg = neg_dest.shape[1]
    slots = cap + neg
    total = stops * (slots + sub)
    total += (-total) % (2 * UNROLL)
    origin = (lax.axis_index("blk") - jnp.arange(stops, dtype=jnp.int32)) % stops
    src = jnp.concatenate([source, neg_source], axis=1)
    live = jnp.concatenate(
        [jnp.arange(cap, dtype=jnp.int32)[None, :] < count[:, None], jnp.ones((stops, neg), bool)], axis=1
    )
    pick = (live[:, :, None] & (src[:, :, None] == jnp.arange(sub, dtype=jnp.int32))).astype(jnp.int32)
    earlier = jnp.arange(slots)[:, None] > jnp.arange(slots)[None, :]
    rank = jnp.sum(jnp.where(earlier[None, :, :, None], pick[:, None, :, :], 0), axis=2)
    held = (jnp.sum(pick, axis=1).reshape(-1) + 1) // 2
    before = jnp.arange(stops * sub)[:, None] > jnp.arange(stops * sub)[None, :]
    first = jnp.sum(jnp.where(before, held[None, :], 0), axis=1).reshape(stops, 1, sub)
    where = jnp.sum(pick * (2 * first + rank), axis=2)
    where = jnp.where(live, where, total).reshape(-1)
    group = origin[:, None] * sub + src
    ids = jnp.concatenate([pattern, jnp.full((stops, neg), bank_size, jnp.int32)], axis=1)
    code = (((group << BANK_BITS) | ids) << DEST_BITS) | jnp.concatenate([dest, neg_dest], axis=1)
    hit = where[None, :] == jnp.arange(total, dtype=jnp.int32)[:, None]
    placed = jnp.sum(jnp.where(hit, code.reshape(-1)[None, :] - dest_tiles, 0), axis=1) + dest_tiles
    return placed, jnp.sum(held).reshape(1)


def pair_kernel(list_ref, pairs_ref, bank_ref, d_hbm, g_hbm, dp_ref, sp_ref, d_v, g_v, gt_v, sems):
    cd = pltpu.make_async_copy(d_hbm, d_v.at[pl.ds(0, d_hbm.shape[0])], sems.at[0])
    cg = pltpu.make_async_copy(g_hbm, g_v, sems.at[1])
    cd.start()
    cg.start()
    d_v[pl.ds(d_hbm.shape[0], T)] = jnp.zeros((T, d_v.shape[1]), d_v.dtype)

    def clear(ref):
        def one(i, carry):
            ref[i] = jnp.zeros(ref.shape[1:], ref.dtype)
            return carry

        lax.fori_loop(0, ref.shape[0], one, 0)

    clear(dp_ref)
    clear(sp_ref)
    cd.wait()
    cg.wait()

    def turn(i, carry):
        gt_v[i] = g_v[pl.ds(i * T, T), :].T
        return carry

    lax.fori_loop(0, gt_v.shape[0], turn, 0)
    shifts = lax.broadcasted_iota(jnp.int32, (32, T), 0)

    def bits(index):
        words = bank_ref[index]
        return jnp.concatenate(
            [
                jnp.right_shift(jnp.broadcast_to(words[k : k + 1, :], (32, T)), shifts) & 1
                for k in range(words.shape[0])
            ],
            axis=0,
        )

    def terms(i):
        codes = [list_ref[2 * i], list_ref[2 * i + 1]]
        g = codes[0] >> (DEST_BITS + BANK_BITS)
        p = [code & (2**DEST_BITS - 1) for code in codes]
        ids = [(code >> DEST_BITS) & (2**BANK_BITS - 1) for code in codes]
        zq = g_v[pl.ds(pl.multiple_of(g * T, T), T), :]
        zp = jnp.concatenate([d_v[pl.ds(pl.multiple_of(k * T, T), T), :] for k in p], axis=0)
        s = lax.dot_general(zq, zp, (((1,), (1,)), ((), ())), preferred_element_type=jnp.float32)
        m = jnp.concatenate([bits(k) for k in ids], axis=1)
        r = (m.astype(jnp.float32) - 0.5 - 0.5 * jnp.tanh(0.5 * s)).astype(jnp.bfloat16)
        to_source = jnp.dot(r, zp, preferred_element_type=jnp.float32)
        to_dest = jnp.dot(gt_v[g], r, preferred_element_type=jnp.float32)
        return g, p, to_source, to_dest

    def body(step, carry):
        done = [terms(step * UNROLL + u) for u in range(UNROLL)]
        for g, p, to_source, to_dest in done:
            sp_ref[g] += to_source
            dp_ref[p[0]] += to_dest[:, :T]
            dp_ref[p[1]] += to_dest[:, T:]
        return carry

    lax.fori_loop(0, (pairs_ref[0] + UNROLL - 1) // UNROLL, body, 0)


def pair_sums(lists, pairs, bank, d, g):
    nd, ng = d.shape[0] // T, g.shape[0] // T
    width = d.shape[1]
    return pl.pallas_call(
        pair_kernel,
        out_shape=(
            jax.ShapeDtypeStruct((nd + 1, width, T), jnp.float32),
            jax.ShapeDtypeStruct((ng, T, width), jnp.float32),
        ),
        in_specs=[
            pl.BlockSpec(memory_space=pltpu.SMEM),
            pl.BlockSpec(memory_space=pltpu.SMEM),
            pl.BlockSpec(memory_space=pltpu.VMEM),
            pl.BlockSpec(memory_space=pl.ANY),
            pl.BlockSpec(memory_space=pl.ANY),
        ],
        out_specs=(pl.BlockSpec(memory_space=pltpu.VMEM),) * 2,
        scratch_shapes=[
            pltpu.VMEM(((nd + 1) * T, width), jnp.bfloat16),
            pltpu.VMEM((ng * T, width), jnp.bfloat16),
            pltpu.VMEM((ng, width, T), jnp.bfloat16),
            pltpu.SemaphoreType.DMA((2,)),
        ],
        compiler_params=pltpu.CompilerParams(vmem_limit_bytes=48 << 20),
    )(lists, pairs, bank, d, g)


def reduce_kernel(scale, dp_ref, sp_ref, out_ref, core_buf, z_buf, y_buf, xh_buf, xl_buf, send, recv):
    sub = core_buf.shape[1]
    z, xh, c, xl, y = place()
    to = peers()
    copies = {}

    def push(name, src, dst, peer):
        k = len(copies)
        copies[name] = pltpu.make_async_remote_copy(
            src_ref=src,
            dst_ref=dst,
            send_sem=send.at[k],
            recv_sem=recv.at[k],
            device_id=to[peer],
            device_id_type=MESH,
        )
        copies[name].start()

    def got(name):
        copies[name].wait_recv()

    def s_at(zz, xx, cc):
        return sp_ref.at[pl.ds(blk_of(zz, xx, cc) * sub, sub)]

    def d_at(xx, yy):
        return dp_ref.at[pl.ds(fiber_of(xx, yy) * sub, sub)]

    def add(total, *parts):
        def one(i, carry):
            value = total[i]
            for part in parts:
                value = value + part[i]
            total[i] = value
            return carry

        lax.fori_loop(0, sub, one, 0)

    meet(to)
    push("y0", d_at(0, y + 2), y_buf.at[0], "y+")
    push("y1", d_at(1, y + 2), y_buf.at[1], "y-")
    order = [(2, 0), (2, 1), (1, 1), (3, 0), (1, 0), (3, 1), (0, 0), (0, 1)]
    for n, (dz, xx) in enumerate(order):
        push(f"c{n}", s_at(z + dz, xx, 1 - c), core_buf.at[n], "sib")
    push("y2", d_at(1, y + 1), y_buf.at[2], "y+")
    push("y3", d_at(0, y + 3), y_buf.at[3], "y-")

    def both(n):
        got(f"c{n}")
        dz, xx = order[n]
        add(core_buf.at[n], s_at(z + dz, xx, c))

    both(0)
    push("z0", core_buf.at[0], z_buf.at[0], "z+")
    both(1)
    push("z1", core_buf.at[1], z_buf.at[1], "z-")
    both(2)
    push("z2", core_buf.at[2], z_buf.at[2], "z+")
    both(3)
    push("z3", core_buf.at[3], z_buf.at[3], "z-")
    for n in range(4, 8):
        both(n)
    got("y0")
    add(y_buf.at[0], d_at(0, y + 1))
    push("y4", y_buf.at[0], y_buf.at[4], "y+")
    got("y1")
    add(y_buf.at[1], d_at(1, y + 3))
    push("y5", y_buf.at[1], y_buf.at[5], "y-")
    got("z0")
    add(z_buf.at[0], core_buf.at[4])
    push("z4", z_buf.at[0], z_buf.at[4], "z+")
    got("z1")
    add(z_buf.at[1], core_buf.at[5])
    push("z5", z_buf.at[1], z_buf.at[5], "z-")
    got("y2")
    got("y3")
    add(y_buf.at[2], d_at(1, y))
    add(y_buf.at[3], d_at(0, y))
    got("z2")
    got("z3")
    add(z_buf.at[2], core_buf.at[7])
    add(z_buf.at[3], core_buf.at[6])
    got("y4")
    got("y5")
    add(y_buf.at[2], y_buf.at[5])
    add(y_buf.at[3], y_buf.at[4])
    push("xl", y_buf.at[2 + xl], xl_buf, "xl")
    got("z4")
    got("z5")
    add(z_buf.at[2], z_buf.at[5])
    add(z_buf.at[3], z_buf.at[4])
    push("xh", z_buf.at[2 + xh], xh_buf, "xh")
    got("xl")
    add(xl_buf, y_buf.at[3 - xl])
    got("xh")
    add(xh_buf, z_buf.at[3 - xh])

    def finish(i, carry):
        out_ref[pl.ds(pl.multiple_of(i * T, T), T), :] = (xh_buf[i] + xl_buf[i].T) * scale
        return carry

    lax.fori_loop(0, sub, finish, 0)
    for copy in copies.values():
        copy.wait_send()


def reduce_sums(dp, sp, rows, scale):
    width = sp.shape[2]
    sub = rows // T
    return pl.pallas_call(
        functools.partial(reduce_kernel, scale),
        out_shape=jax.ShapeDtypeStruct((rows, width), jnp.float32),
        in_specs=[pl.BlockSpec(memory_space=pltpu.VMEM)] * 2,
        out_specs=pl.BlockSpec(memory_space=pltpu.VMEM),
        scratch_shapes=[
            pltpu.VMEM((8, sub, T, width), jnp.float32),
            pltpu.VMEM((6, sub, T, width), jnp.float32),
            pltpu.VMEM((6, sub, width, T), jnp.float32),
            pltpu.VMEM((sub, T, width), jnp.float32),
            pltpu.VMEM((sub, width, T), jnp.float32),
            pltpu.SemaphoreType.DMA((22,)),
            pltpu.SemaphoreType.DMA((22,)),
        ],
        compiler_params=pltpu.CompilerParams(
            collective_id=1, has_side_effects=True, vmem_limit_bytes=48 << 20
        ),
    )(dp, sp)


def on_device(
    embedding, tile_dest, tile_source, tile_count, pattern_id, pattern_bank, negative_dest, negative_source
):
    rows = embedding.shape[0]
    d, g = gather(embedding)
    lists, pairs = pair_lists(
        tile_dest[0, 0],
        tile_source[0, 0],
        tile_count[0, 0],
        pattern_id[0, 0],
        negative_dest[0, 0],
        negative_source[0, 0],
        pattern_bank.shape[0],
        d.shape[0] // T,
        rows // T,
    )
    bank = jnp.concatenate([pattern_bank, jnp.zeros_like(pattern_bank[:1])], axis=0)
    dp, sp = pair_sums(lists, pairs, bank, d, g)
    scale = 1.0 / math.sqrt(T * tile_dest.shape[2])
    return reduce_sums(dp, sp, rows, scale)


def solution(mesh):
    in_specs = (
        P(("blk", "fiber"), None),
        P("blk", "fiber", None, None),
        P("blk", "fiber", None, None),
        P("blk", "fiber", None),
        P("blk", "fiber", None, None),
        P(),
        P("blk", "fiber", None, None),
        P("blk", "fiber", None, None),
    )
    out_specs = P(("blk", "fiber"), None)
    return jax.shard_map(
        on_device, mesh=mesh, in_specs=in_specs, out_specs=out_specs, check_vma=False
    )
```

time: 870 us -> 174 us (0.20)
  the two profiles are of different devices: /device:TPU:1 before, /device:TPU:101 now
where the time goes in v1:
time: 174 us
  Pallas kernels  161 us (93%)
  local copies, waits for them, and re-layouts  7.93 us (5%)
  other arithmetic  4.7 us (3%)
    pallas_call x1, Pallas kernels, reduce_sums(): pl.pallas_call(functools.partial(reduce_kernel, scale), out_shape=jax.Sha...  72.1 us
    pallas_call x1, Pallas kernels, pair_sums(): pl.pallas_call(pair_kernel, out_shape=(jax.ShapeDtypeStruct((nd + 1, widt...  58.9 us
    pallas_call x1, Pallas kernels, gather(): pl.pallas_call(gather_kernel, out_shape=(jax.ShapeDtypeStruct((XS * YS *...  30.3 us
    unnamed x7, local copies, waits for them, and re-layouts  4.77 us

profile of v1, /device:TPU:101, one launch (start us, length us, event | category | flops | bytes accessed | tf_op | source)
XLA Modules:
  0.0 174.0 jit_solution(9765061122151801013)
XLA Ops:
  0.0 0.7 iota_compare_fusion.4
  0.7 0.1 copy.24
  0.9 0.8 copy.21
  1.6 0.8 copy.14
  2.4 0.8 fusion.2
  3.2 0.1 sub.28
  3.3 0.1 copy.15
  3.4 0.6 fusion.4
  4.0 0.1 copy.17
  4.1 0.1 add.67
  4.2 0.1 select_reduce_fusion.3
  4.4 0.1 mul.27
  4.4 0.1 copy.18
  4.6 0.1 copy.16
  4.7 2.0 %select_reduce_fusion.1 = s32[16,28,4]{0,2,1:T(4,128)S(1)} fusion(s32[16,28,4]{1,0,2:T(8,128)S(1)} %copy.16, pred[28,28]{1,0:T(8,128)(4,1)S(1)} %iota_compare_fusion.3), kind=kLoop, calls=%fused_computation.2 | loop fusion | flops 98560 | bytes 15120 | tf_op jit(solution)/shard_map/reduce_sum | solution.py:162
  6.7 0.1 select_reduce_fusion.2
  6.8 0.1 copy.23
  6.8 0.1 eq.37
  6.9 0.2 select_reduce_fusion
  7.2 0.9 concatenate.19.bank_ref
  8.1 30.3 %shard_map.82 = (bf16[4096,256]{1,0:T(8,128)(2,1)}, bf16[8192,256]{1,0:T(8,128)(2,1)}) custom-call(bf16[512,256]{1,0:T(8,128)(2,1)} %e_ref.1), custom_call_target="tpu_custom_call" | custom-call | tf_op jit(solution)/shard_map/pallas_call | solution.py:132
  38.4 0.0 copy-start.1
  38.4 1.6 copy-done.1
  39.9 58.9 %shard_map.83 = (f32[33,256,128]{2,1,0:T(8,128)}, f32[64,128,256]{2,1,0:T(8,128)}) custom-call(s32[512]{0:T(512)S(1)} %broadcast_add_fusion.list_ref, s32[1]{0:T(128)} %bitcast.6.pairs_ref, s32[65,4,128]{2,1,0:T(4,128)S(1)} %concatenate.19.bank_ref, bf16[4096,256]{1,0:T(8,128)(2,1)S(1)} %copy-done.1, bf16[8192,256]{1,0:T(8,128)(2,1)} %get-tuple-element.10.g_hbm), custom_call_target="tpu_custom_call" | custom-call | tf_op jit(solution)/shard_map/pallas_call | solution.py:240
  98.9 0.0 copy-start
  98.9 2.2 %copy-done = f32[33,256,128]{2,1,0:T(8,128)S(1)} copy-done((f32[33,256,128]{2,1,0:T(8,128)S(1)}, f32[33,256,128]{2,1,0:T(8,128)}, u32[]{:S(2)}) %copy-start) | copy-done | bytes 4325400
  101.1 72.1 %shard_map.84 = f32[512,256]{1,0:T(8,128)S(1)} custom-call(f32[33,256,128]{2,1,0:T(8,128)S(1)} %copy-done, f32[64,128,256]{2,1,0:T(8,128)} %get-tuple-element.12.sp_ref), custom_call_target="tpu_custom_call" | custom-call | tf_op jit(solution)/shard_map/pallas_call | solution.py:372
  173.2 0.8 copy.26
  (9 shorter events, 0.1 us)
Async XLA Ops:
  38.4 1.6 copy-start.1
  98.9 2.2 %copy-start = (f32[33,256,128]{2,1,0:T(8,128)S(1)}, f32[33,256,128]{2,1,0:T(8,128)}, u32[]{:S(2)}) copy-start(f32[33,256,128]{2,1,0:T(8,128)} %get-tuple-element.11.dp_ref) | copy-start | bytes 12976132

commit v2 on v1

v2 whole, which is shorter than its diff:
```python
import functools
import math

import jax
import jax.numpy as jnp
from jax import lax
from jax.experimental import pallas as pl
from jax.experimental.pallas import tpu as pltpu
from jax.sharding import PartitionSpec as P

ZS, XS, YS = 4, 2, 4
T = 128
MESH = pl.DeviceIdType.MESH
UNROLL = 6
CHUNKS = 2
VMEM_LIMIT = 60 << 20
DEST_BITS, BANK_BITS = 6, 7


def place():
    b, f = lax.axis_index("blk"), lax.axis_index("fiber")
    return b // 4, (b // 2) % 2, b % 2, f // YS, f % YS


def blk_of(z, xh, c):
    return ((z % ZS) * XS + xh) * 2 + c


def fiber_of(xl, y):
    return xl * YS + y % YS


def peers():
    z, xh, c, xl, y = place()
    b, f = blk_of(z, xh, c), fiber_of(xl, y)
    return {
        "sib": (blk_of(z, xh, 1 - c), f),
        "xh": (blk_of(z, 1 - xh, c), f),
        "z+": (blk_of(z + 1, xh, c), f),
        "z-": (blk_of(z + 3, xh, c), f),
        "xl": (b, fiber_of(1 - xl, y)),
        "y+": (b, fiber_of(xl, y + 1)),
        "y-": (b, fiber_of(xl, y + 3)),
    }


def meet(to):
    barrier = pltpu.get_barrier_semaphore()
    for device in to.values():
        pl.semaphore_signal(barrier, inc=1, device_id=device, device_id_type=MESH)
    pl.semaphore_wait(barrier, len(to))


def gather_kernel(e_ref, d_ref, g_ref, send, recv, local):
    rows = e_ref.shape[0]
    part = rows // CHUNKS
    z, xh, c, xl, y = place()
    to = peers()
    copies = {}

    def push(name, h, src, dst, peer):
        k = len(copies)
        copies[name, h] = pltpu.make_async_remote_copy(
            src_ref=src,
            dst_ref=dst,
            send_sem=send.at[k],
            recv_sem=recv.at[k],
            device_id=to[peer],
            device_id_type=MESH,
        )
        copies[name, h].start()

    def got(name, h):
        copies[name, h].wait_recv()

    def e_at(h):
        return e_ref.at[pl.ds(h * part, part)]

    def g_at(zz, xx, h):
        return g_ref.at[pl.ds(blk_of(zz, xx, c) * rows + h * part, part)]

    def d_at(xx, yy, h):
        return d_ref.at[pl.ds(fiber_of(xx, yy) * rows + h * part, part)]

    def pass_g(name, zz, xx, h, peer):
        push(name, h, g_at(zz, xx, h), g_at(zz, xx, h), peer)

    def pass_d(name, xx, yy, h, peer):
        push(name, h, d_at(xx, yy, h), d_at(xx, yy, h), peer)

    keep_d = pltpu.make_async_copy(e_ref, d_ref.at[pl.ds(fiber_of(xl, y) * rows, rows)], local.at[0])
    keep_g = pltpu.make_async_copy(e_ref, g_ref.at[pl.ds(blk_of(z, xh, c) * rows, rows)], local.at[1])
    keep_d.start()
    keep_g.start()
    meet(to)
    for h in range(CHUNKS):
        push("xh", h, e_at(h), g_at(z, xh, h), "xh")
        push("xl", h, e_at(h), d_at(xl, y, h), "xl")
        push("z+", h, e_at(h), g_at(z, xh, h), "z+")
        push("y+", h, e_at(h), d_at(xl, y, h), "y+")
        push("z-", h, e_at(h), g_at(z, xh, h), "z-")
        push("y-", h, e_at(h), d_at(xl, y, h), "y-")
    for h in range(CHUNKS):
        push("s0", h, e_at(h), g_at(z, xh, h), "sib")
    for h in range(CHUNKS):
        got("xl", h)
        pass_d("xl-", 1 - xl, y, h, "y-")
        pass_d("xl+", 1 - xl, y, h, "y+")
        got("xh", h)
        pass_g("xh-", z, 1 - xh, h, "z-")
        pass_g("xh+", z, 1 - xh, h, "z+")
        pass_g("s2", z, 1 - xh, h, "sib")
    for h in range(CHUNKS):
        got("z+", h)
        pass_g("z++", z + 3, xh, h, "z+")
        pass_g("s1", z + 3, xh, h, "sib")
        got("y+", h)
        pass_d("y++", xl, y + 3, h, "y+")
        got("z-", h)
        pass_g("s3", z + 1, xh, h, "sib")
        got("y-", h)
    for h in range(CHUNKS):
        got("xl-", h)
        pass_d("xl--", 1 - xl, y + 1, h, "y-")
        got("xh-", h)
        pass_g("xh--", z + 1, 1 - xh, h, "z-")
        pass_g("s4", z + 1, 1 - xh, h, "sib")
    for h in range(CHUNKS):
        got("xh+", h)
        pass_g("s6", z + 3, 1 - xh, h, "sib")
        got("z++", h)
        pass_g("s5", z + 2, xh, h, "sib")
        got("xh--", h)
        pass_g("s7", z + 2, 1 - xh, h, "sib")
    for h in range(CHUNKS):
        for name in ("xl+", "y++", "xl--", "s0", "s1", "s2", "s3", "s4", "s5", "s6", "s7"):
            got(name, h)
    for copy in copies.values():
        copy.wait_send()
    keep_d.wait()
    keep_g.wait()


def gather(e):
    rows, width = e.shape
    return pl.pallas_call(
        gather_kernel,
        out_shape=(
            jax.ShapeDtypeStruct((XS * YS * rows, width), e.dtype),
            jax.ShapeDtypeStruct((ZS * XS * 2 * rows, width), e.dtype),
        ),
        in_specs=[pl.BlockSpec(memory_space=pl.ANY)],
        out_specs=(pl.BlockSpec(memory_space=pl.ANY),) * 2,
        scratch_shapes=[
            pltpu.SemaphoreType.DMA((22 * CHUNKS,)),
            pltpu.SemaphoreType.DMA((22 * CHUNKS,)),
            pltpu.SemaphoreType.DMA((2,)),
        ],
        compiler_params=pltpu.CompilerParams(collective_id=0, has_side_effects=True),
    )(e)


def pair_kernel(
    dest_ref, source_ref, count_ref, pattern_ref, neg_dest_ref, neg_source_ref,
    bank_hbm, d_hbm, g_hbm, dp_ref, sp_ref,
    list_ref, open_ref, d_v, g_v, gt_v, bank_v, sems,
):
    stops, cap = dest_ref.shape
    neg = neg_dest_ref.shape[1]
    banks = bank_hbm.shape[0]
    sub = g_hbm.shape[0] // T // stops
    empty = d_hbm.shape[0] // T
    loads = [
        pltpu.make_async_copy(d_hbm, d_v.at[pl.ds(0, d_hbm.shape[0])], sems.at[0]),
        pltpu.make_async_copy(g_hbm, g_v, sems.at[1]),
        pltpu.make_async_copy(bank_hbm, bank_v.at[pl.ds(0, banks)], sems.at[2]),
    ]
    for load in loads:
        load.start()
    d_v[pl.ds(d_hbm.shape[0], T)] = jnp.zeros((T, d_v.shape[1]), d_v.dtype)
    bank_v[banks] = jnp.zeros(bank_v.shape[1:], bank_v.dtype)

    def clear(ref):
        def one(i, carry):
            ref[i] = jnp.zeros(ref.shape[1:], ref.dtype)
            return carry

        lax.fori_loop(0, ref.shape[0], one, 0)

    clear(dp_ref)
    clear(sp_ref)

    b = lax.axis_index("blk")

    def add_slot(pairs, group, src, code):
        held = open_ref[src]
        fresh = held < 0
        list_ref[jnp.where(fresh, 2 * pairs, held)] = code | (group << (DEST_BITS + BANK_BITS))
        open_ref[src] = jnp.where(fresh, 2 * pairs + 1, -1)
        return pairs + fresh.astype(jnp.int32)

    def preset(i, carry):
        list_ref[i] = empty
        return carry

    lax.fori_loop(0, list_ref.shape[0], preset, 0, unroll=8)

    def add_stop(stop, pairs):
        group = lax.rem(b - stop + stops, stops) * sub
        for q in range(sub):
            open_ref[q] = -1
        for k in range(neg):
            src = neg_source_ref[stop, k]
            pairs = add_slot(pairs, group + src, src, (banks << DEST_BITS) | neg_dest_ref[stop, k])

        def listed(k, pairs):
            src = source_ref[stop, k]
            return add_slot(pairs, group + src, src, (pattern_ref[stop, k] << DEST_BITS) | dest_ref[stop, k])

        return lax.fori_loop(0, count_ref[stop], listed, pairs)

    pairs = lax.fori_loop(0, stops, add_stop, 0)
    for load in loads:
        load.wait()

    def turn(i, carry):
        gt_v[i] = g_v[pl.ds(i * T, T), :].T
        return carry

    lax.fori_loop(0, gt_v.shape[0], turn, 0)
    one_bit = jnp.left_shift(1, lax.broadcasted_iota(jnp.int32, (32, T), 0))

    def mask_less_half(index):
        words = bank_v[index]
        return jnp.concatenate(
            [
                jnp.where((jnp.broadcast_to(words[k : k + 1, :], (32, T)) & one_bit) != 0, 0.5, -0.5)
                for k in range(words.shape[0])
            ],
            axis=0,
        )

    def first(i):
        codes = [list_ref[2 * i], list_ref[2 * i + 1]]
        g = codes[0] >> (DEST_BITS + BANK_BITS)
        p = [code & (2**DEST_BITS - 1) for code in codes]
        ids = [(code >> DEST_BITS) & (2**BANK_BITS - 1) for code in codes]
        zq = g_v[pl.ds(pl.multiple_of(g * T, T), T), :]
        zp = jnp.concatenate([d_v[pl.ds(pl.multiple_of(k * T, T), T), :] for k in p], axis=0)
        s = lax.dot_general(zq, zp, (((1,), (1,)), ((), ())), preferred_element_type=jnp.float32)
        m = jnp.concatenate([mask_less_half(k) for k in ids], axis=1)
        r = (m - 0.5 * jnp.tanh(0.5 * s)).astype(jnp.bfloat16)
        return g, p, zp, r

    def second(g, p, zp, r):
        to_source = jnp.dot(r, zp, preferred_element_type=jnp.float32)
        to_dest = jnp.dot(gt_v[g], r, preferred_element_type=jnp.float32)
        sp_ref[g] += to_source
        dp_ref[p[0]] += to_dest[:, :T]
        dp_ref[p[1]] += to_dest[:, T:]

    def body(step, carry):
        for held in [first(step * UNROLL + u) for u in range(UNROLL)]:
            second(*held)
        return carry

    lax.fori_loop(0, (pairs + UNROLL - 1) // UNROLL, body, 0)


def pair_sums(dest, source, count, pattern, neg_dest, neg_source, bank, d, g):
    nd, ng = d.shape[0] // T, g.shape[0] // T
    width = d.shape[1]
    stops, cap = dest.shape
    sub = ng // stops
    most = stops * ((cap + neg_dest.shape[1] + sub) // 2) + UNROLL
    smem = pl.BlockSpec(memory_space=pltpu.SMEM)
    hbm = pl.BlockSpec(memory_space=pl.ANY)
    return pl.pallas_call(
        pair_kernel,
        out_shape=(
            jax.ShapeDtypeStruct((nd + 1, width, T), jnp.float32),
            jax.ShapeDtypeStruct((ng, T, width), jnp.float32),
        ),
        in_specs=[smem] * 6 + [hbm] * 3,
        out_specs=(pl.BlockSpec(memory_space=pltpu.VMEM),) * 2,
        scratch_shapes=[
            pltpu.SMEM((2 * most,), jnp.int32),
            pltpu.SMEM((sub,), jnp.int32),
            pltpu.VMEM(((nd + 1) * T, width), jnp.bfloat16),
            pltpu.VMEM((ng * T, width), jnp.bfloat16),
            pltpu.VMEM((ng, width, T), jnp.bfloat16),
            pltpu.VMEM((bank.shape[0] + 1,) + bank.shape[1:], bank.dtype),
            pltpu.SemaphoreType.DMA((3,)),
        ],
        compiler_params=pltpu.CompilerParams(vmem_limit_bytes=VMEM_LIMIT),
    )(dest, source, count, pattern, neg_dest, neg_source, bank, d, g)


def code16(value_at, blocks, dst, amax):
    height = (dst.shape[0] - 16) // blocks
    power = jnp.ceil(jnp.log2(jnp.maximum(amax, 1e-37)))
    gain = jnp.exp2(-power) * 32767.0

    def one(i, carry):
        q = jnp.clip(jnp.round(value_at(i) * gain), -32767.0, 32767.0)
        dst[pl.ds(pl.multiple_of(i * height, height), height), :] = q.astype(jnp.int32).astype(jnp.int16)
        return carry

    lax.fori_loop(0, blocks, one, 0)
    dst[pl.ds(blocks * height, 16), :] = jnp.broadcast_to(power, (16, power.shape[1])).astype(jnp.int32).astype(jnp.int16)


def reduce_kernel(
    scale, dp_hbm, sp_hbm, out_ref,
    dest, own, core, s_send, s_recv, d_send, d_recv, send, recv, local,
):
    sub = own.shape[1]
    width = own.shape[3]
    per = sub // CHUNKS
    z, xh, c, xl, y = place()
    to = peers()
    copies = {}

    def push(name, src, dst, peer):
        k = len(copies)
        copies[name] = pltpu.make_async_remote_copy(
            src_ref=src,
            dst_ref=dst,
            send_sem=send.at[k],
            recv_sem=recv.at[k],
            device_id=to[peer],
            device_id_type=MESH,
        )
        copies[name].start()

    def got(name):
        copies[name].wait_recv()

    order = [(2, 0), (2, 1), (1, 1), (3, 0), (1, 0), (3, 1), (0, 0), (0, 1)]
    dest_loads, own_loads = [], []
    for n, (dy, xx) in enumerate(order):
        first = pl.ds(fiber_of(xx, y + dy) * sub, sub)
        dest_loads.append(pltpu.make_async_copy(dp_hbm.at[first], dest.at[n], local.at[n]))
        dest_loads[-1].start()
    for n, (dz, xx) in enumerate(order):
        first = pl.ds(blk_of(z + dz, xx, c) * sub, sub)
        own_loads.append(pltpu.make_async_copy(sp_hbm.at[first], own.at[n], local.at[8 + n]))
        own_loads[-1].start()
    meet(to)
    for n, (dz, xx) in enumerate(order):
        first = pl.ds(blk_of(z + dz, xx, 1 - c) * sub, sub)
        push(f"c{n}", sp_hbm.at[first], core.at[n], "sib")

    def decoded(ref, h, height):
        gain = jnp.exp2(ref[h, pl.ds(per * height, 16), :].astype(jnp.float32)[:1]) * (1.0 / 32767.0)

        def at(i):
            rows = pl.ds(pl.multiple_of(i * height, height), height)
            return ref[h, rows, :].astype(jnp.float32) * gain

        return at

    def plain(ref, h):
        return lambda i: ref[h * per + i]

    def total(parts, keep, h):
        def one(i, most):
            value = parts[0](i)
            for part in parts[1:]:
                value = value + part(i)
            keep[h * per + i] = value
            return jnp.maximum(most, jnp.max(jnp.abs(value), axis=0, keepdims=True))

        return lax.fori_loop(0, per, one, jnp.zeros((1, keep.shape[2]), jnp.float32))

    def hand_on(name, parts, keep, h, out_buf, in_buf, peer):
        amax = total(parts, keep, h)
        code16(plain(keep, h), per, out_buf.at[h], amax)
        push(name + str(h), out_buf.at[h], in_buf.at[h], peer)

    def z_send(k, h, peer, *parts):
        hand_on(f"z{k}", parts, core.at[k], h, s_send.at[k], s_recv.at[k], peer)

    def y_send(k, h, peer, *parts):
        hand_on(f"y{k}", parts, dest.at[k], h, d_send.at[k], d_recv.at[k], peer)

    def s_in(name, k, h):
        got(name + str(h))
        return decoded(s_recv.at[k], h, T)

    def d_in(name, k, h):
        got(name + str(h))
        return decoded(d_recv.at[k], h, width)

    def cores(n, h):
        return plain(core.at[n], h), plain(own.at[n], h)

    def ready(n):
        own_loads[n].wait()
        got(f"c{n}")

    dest_loads[0].wait()
    y_send(0, 0, "y+", plain(dest.at[0], 0))
    dest_loads[1].wait()
    y_send(1, 0, "y-", plain(dest.at[1], 0))
    ready(0)
    z_send(0, 0, "z+", *cores(0, 0))
    ready(1)
    z_send(1, 0, "z-", *cores(1, 0))
    ready(2)
    ready(3)
    dest_loads[2].wait()
    dest_loads[3].wait()
    for h in range(CHUNKS):
        if h:
            y_send(0, h, "y+", plain(dest.at[0], h))
            y_send(1, h, "y-", plain(dest.at[1], h))
            z_send(0, h, "z+", *cores(0, h))
            z_send(1, h, "z-", *cores(1, h))
        else:
            y_send(2, h, "y+", plain(dest.at[2], h))
            y_send(3, h, "y-", plain(dest.at[3], h))
            z_send(2, h, "z+", *cores(2, h))
            z_send(3, h, "z-", *cores(3, h))
    for n in range(4, 8):
        ready(n)
        dest_loads[n].wait()
    for h in range(CHUNKS):
        y_send(4, h, "y+", plain(dest.at[4], h), d_in("y0", 0, h))
        y_send(5, h, "y-", plain(dest.at[5], h), d_in("y1", 1, h))
        z_send(4, h, "z+", *cores(4, h), s_in("z0", 0, h))
        z_send(5, h, "z-", *cores(5, h), s_in("z1", 1, h))
    for h in range(1, CHUNKS):
        y_send(2, h, "y+", plain(dest.at[2], h))
        y_send(3, h, "y-", plain(dest.at[3], h))
        z_send(2, h, "z+", *cores(2, h))
        z_send(3, h, "z-", *cores(3, h))
    for h in range(CHUNKS):
        most_d = [
            total((plain(dest.at[6], h), d_in("y3", 3, h), d_in("y4", 4, h)), dest.at[6], h),
            total((plain(dest.at[7], h), d_in("y2", 2, h), d_in("y5", 5, h)), dest.at[7], h),
        ]
        code16(plain(dest.at[7 - xl], h), per, d_send.at[6, h], jnp.where(xl == 0, most_d[1], most_d[0]))
        push(f"xl{h}", d_send.at[6, h], d_recv.at[6, h], "xl")
        most_s = [
            total((*cores(6, h), s_in("z3", 3, h), s_in("z4", 4, h)), core.at[6], h),
            total((*cores(7, h), s_in("z2", 2, h), s_in("z5", 5, h)), core.at[7], h),
        ]
        code16(plain(core.at[7 - xh], h), per, s_send.at[6, h], jnp.where(xh == 0, most_s[1], most_s[0]))
        push(f"xh{h}", s_send.at[6, h], s_recv.at[6, h], "xh")
    for h in range(CHUNKS):
        from_xl = d_in("xl", 6, h)
        from_xh = s_in("xh", 6, h)

        def finish(i, carry):
            by_dest = dest[6 + xl, h * per + i] + from_xl(i)
            by_source = core[6 + xh, h * per + i] + from_xh(i)
            rows = pl.ds(pl.multiple_of((h * per + i) * T, T), T)
            out_ref[rows, :] = (by_source + by_dest.T) * scale
            return carry

        lax.fori_loop(0, per, finish, 0)
    for copy in copies.values():
        copy.wait_send()


def reduce_sums(dp, sp, rows, scale):
    width = sp.shape[2]
    sub = rows // T
    per = sub // CHUNKS
    return pl.pallas_call(
        functools.partial(reduce_kernel, scale),
        out_shape=jax.ShapeDtypeStruct((rows, width), jnp.float32),
        in_specs=[pl.BlockSpec(memory_space=pl.ANY)] * 2,
        out_specs=pl.BlockSpec(memory_space=pltpu.VMEM),
        scratch_shapes=[
            pltpu.VMEM((8, sub, width, T), jnp.float32),
            pltpu.VMEM((8, sub, T, width), jnp.float32),
            pltpu.VMEM((8, sub, T, width), jnp.float32),
            pltpu.VMEM((7, CHUNKS, per * T + 16, width), jnp.int16),
            pltpu.VMEM((7, CHUNKS, per * T + 16, width), jnp.int16),
            pltpu.VMEM((7, CHUNKS, per * width + 16, T), jnp.int16),
            pltpu.VMEM((7, CHUNKS, per * width + 16, T), jnp.int16),
            pltpu.SemaphoreType.DMA((8 + 14 * CHUNKS,)),
            pltpu.SemaphoreType.DMA((8 + 14 * CHUNKS,)),
            pltpu.SemaphoreType.DMA((16,)),
        ],
        compiler_params=pltpu.CompilerParams(
            collective_id=1, has_side_effects=True, vmem_limit_bytes=VMEM_LIMIT
        ),
    )(dp, sp)


def on_device(
    embedding, tile_dest, tile_source, tile_count, pattern_id, pattern_bank, negative_dest, negative_source
):
    rows = embedding.shape[0]
    d, g = gather(embedding)
    dp, sp = pair_sums(
        tile_dest[0, 0],
        tile_source[0, 0],
        tile_count[0, 0],
        pattern_id[0, 0],
        negative_dest[0, 0],
        negative_source[0, 0],
        pattern_bank,
        d,
        g,
    )
    scale = 1.0 / math.sqrt(T * tile_dest.shape[2])
    return reduce_sums(dp, sp, rows, scale)


def solution(mesh):
    in_specs = (
        P(("blk", "fiber"), None),
        P("blk", "fiber", None, None),
        P("blk", "fiber", None, None),
        P("blk", "fiber", None),
        P("blk", "fiber", None, None),
        P(),
        P("blk", "fiber", None, None),
        P("blk", "fiber", None, None),
    )
    out_specs = P(("blk", "fiber"), None)
    return jax.shard_map(
        on_device, mesh=mesh, in_specs=in_specs, out_specs=out_specs, check_vma=False
    )
```

time: 174 us -> 110 us (0.63)
  the two profiles are of different devices: /device:TPU:101 before, /device:TPU:32 now
where the time goes in v2:
time: 110 us
  Pallas kernels  105 us (95%)
  local copies, waits for them, and re-layouts  4.57 us (4%)
    pallas_call x1, Pallas kernels, reduce_sums(): pl.pallas_call(functools.partial(reduce_kernel, scale), out_shape=jax.Sha...  41.1 us
    pallas_call x1, Pallas kernels, pair_sums(): pl.pallas_call(pair_kernel, out_shape=(jax.ShapeDtypeStruct((nd + 1, widt...  34.2 us
    pallas_call x1, Pallas kernels, gather(): pl.pallas_call(gather_kernel, out_shape=(jax.ShapeDtypeStruct((XS * YS *...  30.1 us

profile of v2, /device:TPU:32, one launch (start us, length us, event | category | flops | bytes accessed | tf_op | source)
XLA Modules:
  0.0 110.0 jit_solution(1885458286596596797)
XLA Ops:
  0.0 1.4 %copy.9.neg_dest_ref = s32[16,4]{1,0:T(8,128)} copy(s32[16,4]{0,1:T(4,128)} %bitcast.9) | data formatting | bytes 512 | tf_op jit(solution)/shard_map/squeeze | solution.py:504
  1.4 1.4 %copy.10.neg_source_ref = s32[16,4]{1,0:T(8,128)} copy(s32[16,4]{0,1:T(4,128)} %bitcast.10) | data formatting | bytes 512 | tf_op jit(solution)/shard_map/squeeze | solution.py:505
  2.7 30.1 %shard_map.82 = (bf16[4096,256]{1,0:T(8,128)(2,1)}, bf16[8192,256]{1,0:T(8,128)(2,1)}) custom-call(bf16[512,256]{1,0:T(8,128)(2,1)} %e_ref.1), custom_call_target="tpu_custom_call" | custom-call | tf_op jit(solution)/shard_map/pallas_call | solution.py:146
  32.8 34.2 %shard_map.83 = (f32[33,256,128]{2,1,0:T(8,128)}, f32[64,128,256]{2,1,0:T(8,128)}) custom-call(s32[16,24]{1,0:T(8,128)} %bitcast.6, s32[16,24]{1,0:T(8,128)} %bitcast.7, s32[16]{0:T(128)} %bitcast.11, s32[16,24]{1,0:T(8,128)} %bitcast.8, s32[16,4]{1,0:T(8,128)} %copy.9.neg_dest_ref, s32[16,4]{1,0:T(8,128)} %copy.10.neg_source_ref, s32[64,4,128]{2,1,0:T(4,128)} %bank_hbm.1, ...), custom_call_target="tpu_custom_call" | custom-call | tf_op jit(solution)/shard_map/pallas_call | solution.py:278
  67.1 41.1 %shard_map.84 = f32[512,256]{1,0:T(8,128)} custom-call(f32[33,256,128]{2,1,0:T(8,128)} %get-tuple-element.11.dp_hbm, f32[64,128,256]{2,1,0:T(8,128)} %get-tuple-element.12.sp_hbm), custom_call_target="tpu_custom_call" | custom-call | tf_op jit(solution)/shard_map/pallas_call | solution.py:471
  108.2 1.9 %copy.12 = f32[512,256]{1,0:T(8,128)} copy(f32[512,256]{1,0:T(8,128)} %shard_map.84) | data formatting | bytes 1048576

commit v3 on v2

v3 whole, which is shorter than its diff:
```python
import functools
import math

import jax
import jax.numpy as jnp
from jax import lax
from jax.experimental import pallas as pl
from jax.experimental.pallas import tpu as pltpu
from jax.sharding import PartitionSpec as P

ZS, XS, YS = 4, 2, 4
T = 128
MESH = pl.DeviceIdType.MESH
UNROLL = 6
CHUNKS = 2
PARTS = 4
PAIR_VMEM, REDUCE_VMEM = 30, 36
DEST_BITS, BANK_BITS = 6, 7


def place():
    b, f = lax.axis_index("blk"), lax.axis_index("fiber")
    return b // 4, (b // 2) % 2, b % 2, f // YS, f % YS


def blk_of(z, xh, c):
    return ((z % ZS) * XS + xh) * 2 + c


def fiber_of(xl, y):
    return xl * YS + y % YS


def peers():
    z, xh, c, xl, y = place()
    b, f = blk_of(z, xh, c), fiber_of(xl, y)
    return {
        "sib": (blk_of(z, xh, 1 - c), f),
        "xh": (blk_of(z, 1 - xh, c), f),
        "z+": (blk_of(z + 1, xh, c), f),
        "z-": (blk_of(z + 3, xh, c), f),
        "xl": (b, fiber_of(1 - xl, y)),
        "y+": (b, fiber_of(xl, y + 1)),
        "y-": (b, fiber_of(xl, y + 3)),
    }


def meet(to):
    barrier = pltpu.get_barrier_semaphore()
    for device in to.values():
        pl.semaphore_signal(barrier, inc=1, device_id=device, device_id_type=MESH)
    pl.semaphore_wait(barrier, len(to))


def gather_kernel(e_ref, d_ref, g_ref, send, recv, local):
    rows = e_ref.shape[0]
    part = rows // PARTS
    z, xh, c, xl, y = place()
    to = peers()
    copies = {}

    def push(name, src, dst, peer):
        k = len(copies)
        copies[name] = pltpu.make_async_remote_copy(
            src_ref=src,
            dst_ref=dst,
            send_sem=send.at[k],
            recv_sem=recv.at[k],
            device_id=to[peer],
            device_id_type=MESH,
        )
        copies[name].start()

    def got(name, h):
        copies[name, h].wait_recv()

    def e_at(h):
        return e_ref.at[pl.ds(h * part, part)]

    def g_at(zz, xx, h):
        return g_ref.at[pl.ds(blk_of(zz, xx, c) * rows + h * part, part)]

    def d_at(xx, yy, h):
        return d_ref.at[pl.ds(fiber_of(xx, yy) * rows + h * part, part)]

    def pass_g(name, zz, xx, h, peer):
        push((name, h), g_at(zz, xx, h), g_at(zz, xx, h), peer)

    def pass_d(name, xx, yy, h, peer):
        push((name, h), d_at(xx, yy, h), d_at(xx, yy, h), peer)

    def share(zz, xx, src=None):
        whole = g_ref.at[pl.ds(blk_of(zz, xx, c) * rows, rows)]
        push(("sib", len(copies)), whole if src is None else src, whole, "sib")

    keep_d = pltpu.make_async_copy(e_ref, d_ref.at[pl.ds(fiber_of(xl, y) * rows, rows)], local.at[0])
    keep_g = pltpu.make_async_copy(e_ref, g_ref.at[pl.ds(blk_of(z, xh, c) * rows, rows)], local.at[1])
    keep_d.start()
    keep_g.start()
    meet(to)
    for h in range(PARTS):
        push(("xh", h), e_at(h), g_at(z, xh, h), "xh")
        push(("xl", h), e_at(h), d_at(xl, y, h), "xl")
        push(("z+", h), e_at(h), g_at(z, xh, h), "z+")
        push(("y+", h), e_at(h), d_at(xl, y, h), "y+")
        push(("z-", h), e_at(h), g_at(z, xh, h), "z-")
        push(("y-", h), e_at(h), d_at(xl, y, h), "y-")

    def second_hop(h):
        got("xl-", h)
        pass_d("xl--", 1 - xl, y + 1, h, "y-")
        got("xh-", h)
        pass_g("xh--", z + 1, 1 - xh, h, "z-")

    for h in range(PARTS):
        got("z+", h)
        pass_g("z++", z + 3, xh, h, "z+")
        got("y+", h)
        pass_d("y++", xl, y + 3, h, "y+")
        got("xl", h)
        pass_d("xl-", 1 - xl, y, h, "y-")
        pass_d("xl+", 1 - xl, y, h, "y+")
        got("xh", h)
        pass_g("xh-", z, 1 - xh, h, "z-")
        pass_g("xh+", z, 1 - xh, h, "z+")
        if h:
            second_hop(h - 1)
    share(z, xh, e_ref)
    share(z + 3, xh)
    share(z, 1 - xh)
    second_hop(PARTS - 1)
    share(z + 1, 1 - xh)
    for name, zz, xx in (("z-", z + 1, xh), ("z++", z + 2, xh), ("xh+", z + 3, 1 - xh), ("xh--", z + 2, 1 - xh)):
        for h in range(PARTS):
            got(name, h)
        share(zz, xx)
    for h in range(PARTS):
        for name in ("y-", "xl+", "y++", "xl--"):
            got(name, h)
    for (name, _), copy in copies.items():
        if name == "sib":
            copy.wait_recv()
    for copy in copies.values():
        copy.wait_send()
    keep_d.wait()
    keep_g.wait()


def gather(e):
    rows, width = e.shape
    copies = 14 * PARTS + 8
    return pl.pallas_call(
        gather_kernel,
        out_shape=(
            jax.ShapeDtypeStruct((XS * YS * rows, width), e.dtype),
            jax.ShapeDtypeStruct((ZS * XS * 2 * rows, width), e.dtype),
        ),
        in_specs=[pl.BlockSpec(memory_space=pl.ANY)],
        out_specs=(pl.BlockSpec(memory_space=pl.ANY),) * 2,
        scratch_shapes=[
            pltpu.SemaphoreType.DMA((copies,)),
            pltpu.SemaphoreType.DMA((copies,)),
            pltpu.SemaphoreType.DMA((2,)),
        ],
        compiler_params=pltpu.CompilerParams(
            collective_id=0, has_side_effects=True, vmem_limit_bytes=4 << 20
        ),
    )(e)


def pair_kernel(
    dest_ref, source_ref, count_ref, pattern_ref, neg_dest_ref, neg_source_ref, bank_ref, d_ref, g_ref,
    dp_ref, sp_ref, list_ref, open_ref, gt_v,
):
    stops, cap = dest_ref.shape[2:]
    neg = neg_dest_ref.shape[2]
    sub = sp_ref.shape[0] // stops
    per = dp_ref.shape[0] // stops
    dump = list_ref.shape[0] - 1
    b = lax.axis_index("blk")

    def preset(i, carry):
        list_ref[i] = 0
        return carry

    lax.fori_loop(0, list_ref.shape[0], preset, 0, unroll=16)

    def add_slot(pairs, src, code, live):
        held = open_ref[src]
        fresh = held < 0
        at = jnp.where(fresh, 2 * pairs, held)
        list_ref[jnp.where(live, at, dump)] = (code << 2) | 2
        open_ref[src] = jnp.where(live, jnp.where(fresh, 2 * pairs + 1, -1), held)
        return pairs + jnp.where(live & fresh, 1, 0)

    def add_stop(stop, pairs):
        group = lax.rem(b - stop + stops, stops) * sub
        count = count_ref[0, 0, stop]
        for q in range(sub):
            open_ref[q] = -1
            tile = stop * sub + q
            gt_v[tile] = g_ref[pl.ds(pl.multiple_of(tile * T, T), T), :].T
            sp_ref[tile] = jnp.zeros(sp_ref.shape[1:], sp_ref.dtype)
        for q in range(per):
            dp_ref[stop * per + q] = jnp.zeros(dp_ref.shape[1:], dp_ref.dtype)

        def code(src, index, dest, negative):
            return ((((group + src) << BANK_BITS) | index) << DEST_BITS | dest) << 1 | negative

        for k in range(neg):
            src = neg_source_ref[0, 0, k, stop]
            pairs = add_slot(pairs, src, code(src, 0, neg_dest_ref[0, 0, k, stop], 1), True)
        for k in range(cap):
            src = source_ref[0, 0, stop, k]
            value = code(src, pattern_ref[0, 0, stop, k], dest_ref[0, 0, stop, k], 0)
            pairs = add_slot(pairs, src, value, k < count)
        return pairs

    pairs = lax.fori_loop(0, stops, add_stop, 0)
    one_bit = jnp.left_shift(1, lax.broadcasted_iota(jnp.int32, (32, T), 0))

    def mask_less_half(index, keep):
        words = bank_ref[index] & keep
        return jnp.concatenate(
            [
                jnp.where((jnp.broadcast_to(words[k : k + 1, :], (32, T)) & one_bit) != 0, 0.5, -0.5)
                for k in range(words.shape[0])
            ],
            axis=0,
        )

    def first(i):
        codes = [list_ref[2 * i], list_ref[2 * i + 1]]
        g = codes[0] >> (DEST_BITS + BANK_BITS + 3)
        p = [(code >> 3) & (2**DEST_BITS - 1) for code in codes]
        ids = [(code >> (DEST_BITS + 3)) & (2**BANK_BITS - 1) for code in codes]
        keep = [((code >> 2) & 1) - 1 for code in codes]
        live = [((code >> 1) & 1).astype(jnp.float32) for code in codes]
        zq = g_ref[pl.ds(pl.multiple_of(g * T, T), T), :]
        zp = jnp.concatenate([d_ref[pl.ds(pl.multiple_of(k * T, T), T), :] for k in p], axis=0)
        s = lax.dot_general(zq, zp, (((1,), (1,)), ((), ())), preferred_element_type=jnp.float32)
        half = 0.5 * jnp.tanh(0.5 * s)
        r = jnp.concatenate(
            [live[u] * (mask_less_half(ids[u], keep[u]) - half[:, u * T : (u + 1) * T]) for u in range(2)], axis=1
        ).astype(jnp.bfloat16)
        return g, p, zp, r

    def second(g, p, zp, r):
        to_source = jnp.dot(r, zp, preferred_element_type=jnp.float32)
        to_dest = jnp.dot(gt_v[g], r, preferred_element_type=jnp.float32)
        sp_ref[g] += to_source
        dp_ref[p[0]] += to_dest[:, :T]
        dp_ref[p[1]] += to_dest[:, T:]

    def body(step, carry):
        for held in [first(step * UNROLL + u) for u in range(UNROLL)]:
            second(*held)
        return carry

    lax.fori_loop(0, (pairs + UNROLL - 1) // UNROLL, body, 0)


def pair_sums(dest, source, count, pattern, neg_dest, neg_source, bank, d, g):
    nd, ng = d.shape[0] // T, g.shape[0] // T
    width = d.shape[1]
    stops, cap = dest.shape[2:]
    sub = ng // stops
    most = stops * ((cap + neg_dest.shape[2] + sub) // 2) + UNROLL
    most += (-most) % 8 + 8
    smem = pl.BlockSpec(memory_space=pltpu.SMEM)
    vmem = pl.BlockSpec(memory_space=pltpu.VMEM)
    return pl.pallas_call(
        pair_kernel,
        out_shape=(
            jax.ShapeDtypeStruct((nd, width, T), jnp.float32),
            jax.ShapeDtypeStruct((ng, T, width), jnp.float32),
        ),
        in_specs=[smem] * 6 + [vmem] * 3,
        out_specs=(vmem, vmem),
        scratch_shapes=[
            pltpu.SMEM((2 * most,), jnp.int32),
            pltpu.SMEM((sub,), jnp.int32),
            pltpu.VMEM((ng, width, T), jnp.bfloat16),
        ],
        compiler_params=pltpu.CompilerParams(vmem_limit_bytes=PAIR_VMEM << 20),
    )(dest, source, count, pattern, neg_dest, neg_source, bank, d, g)


def code16(value_at, blocks, dst, amax):
    height = (dst.shape[0] - 16) // blocks
    power = jnp.ceil(jnp.log2(jnp.maximum(amax, 1e-37)))
    gain = jnp.exp2(-power) * 32767.0

    def one(i, carry):
        q = jnp.clip(jnp.round(value_at(i) * gain), -32767.0, 32767.0)
        dst[pl.ds(pl.multiple_of(i * height, height), height), :] = q.astype(jnp.int32).astype(jnp.int16)
        return carry

    lax.fori_loop(0, blocks, one, 0)
    dst[pl.ds(blocks * height, 16), :] = jnp.broadcast_to(power, (16, power.shape[1])).astype(jnp.int32).astype(jnp.int16)


def reduce_kernel(
    scale, dp_ref, sp_ref, out_ref, dest, core, s_send, s_recv, d_send, d_recv, send, recv
):
    sub = core.shape[1]
    width = core.shape[3]
    per = sub // CHUNKS
    z, xh, c, xl, y = place()
    to = peers()
    copies = {}

    def push(name, src, dst, peer):
        k = len(copies)
        copies[name] = pltpu.make_async_remote_copy(
            src_ref=src,
            dst_ref=dst,
            send_sem=send.at[k],
            recv_sem=recv.at[k],
            device_id=to[peer],
            device_id_type=MESH,
        )
        copies[name].start()

    def got(name):
        copies[name].wait_recv()

    order = [(2, 0), (2, 1), (1, 1), (3, 0), (1, 0), (3, 1), (0, 0), (0, 1)]

    def s_at(n, core_at):
        dz, xx = order[n]
        return sp_ref.at[pl.ds(blk_of(z + dz, xx, core_at) * sub, sub)]

    def mine(n, h):
        dy, xx = order[n]
        return plain(dp_ref.at[pl.ds(fiber_of(xx, y + dy) * sub, sub)], h)

    meet(to)
    for n in range(8):
        push(f"c{n}", s_at(n, 1 - c), core.at[n], "sib")

    def decoded(ref, h, height):
        gain = jnp.exp2(ref[h, pl.ds(per * height, 16), :].astype(jnp.float32)[:1]) * (1.0 / 32767.0)

        def at(i):
            rows = pl.ds(pl.multiple_of(i * height, height), height)
            return ref[h, rows, :].astype(jnp.float32) * gain

        return at

    def plain(ref, h):
        return lambda i: ref[h * per + i]

    def total(parts, keep, h):
        def one(i, most):
            value = parts[0](i)
            for part in parts[1:]:
                value = value + part(i)
            keep[h * per + i] = value
            return jnp.maximum(most, jnp.max(jnp.abs(value), axis=0, keepdims=True))

        return lax.fori_loop(0, per, one, jnp.zeros((1, keep.shape[2]), jnp.float32))

    def hand_on(name, parts, keep, h, out_buf, in_buf, peer):
        amax = total(parts, keep, h)
        code16(plain(keep, h), per, out_buf.at[h], amax)
        push(name + str(h), out_buf.at[h], in_buf.at[h], peer)

    def z_send(k, h, peer, *parts):
        hand_on(f"z{k}", parts, core.at[k], h, s_send.at[k], s_recv.at[k], peer)

    def y_send(k, h, peer, *parts):
        hand_on(f"y{k}", parts, dest.at[k], h, d_send.at[k], d_recv.at[k], peer)

    def s_in(name, k, h):
        got(name + str(h))
        return decoded(s_recv.at[k], h, T)

    def d_in(name, k, h):
        got(name + str(h))
        return decoded(d_recv.at[k], h, width)

    def cores(n, h):
        return plain(core.at[n], h), plain(s_at(n, c), h)

    y_send(0, 0, "y+", mine(0, 0))
    y_send(1, 0, "y-", mine(1, 0))
    got("c0")
    z_send(0, 0, "z+", *cores(0, 0))
    got("c1")
    z_send(1, 0, "z-", *cores(1, 0))
    for h in range(1, CHUNKS):
        y_send(0, h, "y+", mine(0, h))
        y_send(1, h, "y-", mine(1, h))
        z_send(0, h, "z+", *cores(0, h))
        z_send(1, h, "z-", *cores(1, h))
    for n in range(2, 8):
        got(f"c{n}")
    for h in range(CHUNKS):
        y_send(2, h, "y+", mine(2, h))
        y_send(3, h, "y-", mine(3, h))
        z_send(2, h, "z+", *cores(2, h))
        z_send(3, h, "z-", *cores(3, h))
        y_send(4, h, "y+", mine(4, h), d_in("y0", 0, h))
        y_send(5, h, "y-", mine(5, h), d_in("y1", 1, h))
        z_send(4, h, "z+", *cores(4, h), s_in("z0", 0, h))
        z_send(5, h, "z-", *cores(5, h), s_in("z1", 1, h))
    for h in range(CHUNKS):
        most_d = [
            total((mine(6, h), d_in("y3", 3, h), d_in("y4", 4, h)), dest.at[6], h),
            total((mine(7, h), d_in("y2", 2, h), d_in("y5", 5, h)), dest.at[7], h),
        ]
        code16(plain(dest.at[7 - xl], h), per, d_send.at[6, h], jnp.where(xl == 0, most_d[1], most_d[0]))
        push(f"xl{h}", d_send.at[6, h], d_recv.at[6, h], "xl")
        most_s = [
            total((*cores(6, h), s_in("z3", 3, h), s_in("z4", 4, h)), core.at[6], h),
            total((*cores(7, h), s_in("z2", 2, h), s_in("z5", 5, h)), core.at[7], h),
        ]
        code16(plain(core.at[7 - xh], h), per, s_send.at[6, h], jnp.where(xh == 0, most_s[1], most_s[0]))
        push(f"xh{h}", s_send.at[6, h], s_recv.at[6, h], "xh")
    for h in range(CHUNKS):
        from_xl = d_in("xl", 6, h)
        from_xh = s_in("xh", 6, h)

        def finish(i, carry):
            by_dest = dest[6 + xl, h * per + i] + from_xl(i)
            by_source = core[6 + xh, h * per + i] + from_xh(i)
            rows = pl.ds(pl.multiple_of((h * per + i) * T, T), T)
            out_ref[rows, :] = (by_source + by_dest.T) * scale
            return carry

        lax.fori_loop(0, per, finish, 0)
    for copy in copies.values():
        copy.wait_send()


def reduce_sums(dp, sp, rows, scale):
    width = sp.shape[2]
    sub = rows // T
    per = sub // CHUNKS
    return pl.pallas_call(
        functools.partial(reduce_kernel, scale),
        out_shape=jax.ShapeDtypeStruct((rows, width), jnp.float32),
        in_specs=[pl.BlockSpec(memory_space=pltpu.VMEM)] * 2,
        out_specs=pl.BlockSpec(memory_space=pltpu.VMEM),
        scratch_shapes=[
            pltpu.VMEM((8, sub, width, T), jnp.float32),
            pltpu.VMEM((8, sub, T, width), jnp.float32),
            pltpu.VMEM((7, CHUNKS, per * T + 16, width), jnp.int16),
            pltpu.VMEM((7, CHUNKS, per * T + 16, width), jnp.int16),
            pltpu.VMEM((7, CHUNKS, per * width + 16, T), jnp.int16),
            pltpu.VMEM((7, CHUNKS, per * width + 16, T), jnp.int16),
            pltpu.SemaphoreType.DMA((8 + 14 * CHUNKS,)),
            pltpu.SemaphoreType.DMA((8 + 14 * CHUNKS,)),
        ],
        compiler_params=pltpu.CompilerParams(
            collective_id=1, has_side_effects=True, vmem_limit_bytes=REDUCE_VMEM << 20
        ),
    )(dp, sp)


def on_device(
    embedding, tile_dest, tile_source, tile_count, pattern_id, pattern_bank, negative_dest, negative_source
):
    rows = embedding.shape[0]
    d, g = gather(embedding)
    dp, sp = pair_sums(
        tile_dest,
        tile_source,
        tile_count,
        pattern_id,
        negative_dest.swapaxes(2, 3),
        negative_source.swapaxes(2, 3),
        pattern_bank,
        d,
        g,
    )
    scale = 1.0 / math.sqrt(T * tile_dest.shape[2])
    return reduce_sums(dp, sp, rows, scale)


def solution(mesh):
    in_specs = (
        P(("blk", "fiber"), None),
        P("blk", "fiber", None, None),
        P("blk", "fiber", None, None),
        P("blk", "fiber", None),
        P("blk", "fiber", None, None),
        P(),
        P("blk", "fiber", None, None),
        P("blk", "fiber", None, None),
    )
    out_specs = P(("blk", "fiber"), None)
    return jax.shard_map(
        on_device, mesh=mesh, in_specs=in_specs, out_specs=out_specs, check_vma=False
    )
```

time: 110 us -> 99.2 us (0.902)
  the two profiles are of different devices: /device:TPU:32 before, /device:TPU:1 now
where the time goes in v3:
time: 99.2 us; the launch traced here: 98.9 us
  Pallas kernels  92.1 us (93%)
  local copies, waits for them, and re-layouts  6.75 us (7%)
    pallas_call x1, Pallas kernels, reduce_sums(): pl.pallas_call(functools.partial(reduce_kernel, scale), out_shape=jax.Sha...  42.4 us
    pallas_call x1, Pallas kernels, gather(): pl.pallas_call(gather_kernel, out_shape=(jax.ShapeDtypeStruct((XS * YS *...  29.4 us
    pallas_call x1, Pallas kernels, pair_sums(): pl.pallas_call(pair_kernel, out_shape=(jax.ShapeDtypeStruct((nd, width, T...  20.3 us
    unnamed x17, local copies, waits for them, and re-layouts  6.75 us

profile of v3, /device:TPU:1, one launch (start us, length us, event | category | flops | bytes accessed | tf_op | source)
XLA Modules:
  0.0 98.9 jit_solution(15299332940062283988)
XLA Ops:
  0.0 0.0 copy-start
  0.0 0.9 copy-done
  1.0 29.4 %shard_map.82 = (bf16[4096,256]{1,0:T(8,128)(2,1)S(1)}, bf16[8192,256]{1,0:T(8,128)(2,1)S(1)}) custom-call(bf16[512,256]{1,0:T(8,128)(2,1)S(1)} %copy-done), custom_call_target="tpu_custom_call" | custom-call | tf_op jit(solution)/shard_map/pallas_call | solution.py:152
  30.4 0.0 copy-start.1
  30.4 0.9 copy-done.1
  31.3 0.0 copy-start.2
  31.3 0.7 copy-done.2
  32.0 0.0 copy-start.3
  32.0 0.7 copy-done.3
  32.7 0.0 copy-start.4
  32.7 0.7 copy-done.4
  33.4 0.0 copy-start.5
  33.4 0.7 copy-done.5
  34.1 0.0 copy-start.6
  34.1 0.7 copy-done.6
  34.7 0.0 copy-start.7
  34.7 0.7 copy-done.7
  35.4 20.3 %shard_map.83 = (f32[32,256,128]{2,1,0:T(8,128)S(1)}, f32[64,128,256]{2,1,0:T(8,128)S(1)}) custom-call(s32[1,1,16,24]{3,2,1,0:T(8,128)S(1)} %copy-done.2, s32[1,1,16,24]{3,2,1,0:T(8,128)S(1)} %copy-done.3, s32[1,1,16]{2,1,0:T(1,128)S(1)} %copy-done.7, s32[1,1,16,24]{3,2,1,0:T(8,128)S(1)} %copy-done.4, s32[1,1,4,16]{3,2,1,0:T(4,128)S(1)} %bitcast.2, ...), custom_call_target="tpu_custom_call" | custom-call | tf_op jit(solution)/shard_map/pallas_call | solution.py:272
  55.7 42.4 %shard_map.84 = f32[512,256]{1,0:T(8,128)S(1)} custom-call(f32[32,256,128]{2,1,0:T(8,128)S(1)} %get-tuple-element.11.dp_ref, f32[64,128,256]{2,1,0:T(8,128)S(1)} %get-tuple-element.12.sp_ref), custom_call_target="tpu_custom_call" | custom-call | tf_op jit(solution)/shard_map/pallas_call | solution.py:441
  98.1 0.8 copy.10
Async XLA Ops:
  0.0 0.9 copy-start
  30.4 0.9 copy-start.1
  31.3 0.7 copy-start.2
  32.0 0.7 copy-start.3
  32.7 0.7 copy-start.4
  33.4 0.7 copy-start.5
  34.1 0.7 copy-start.6
  34.7 0.7 copy-start.7

commit v4 on v3

--- a/solution.py
+++ b/solution.py
@@ -12,10 +12,13 @@
 T = 128
 MESH = pl.DeviceIdType.MESH
 UNROLL = 6
-CHUNKS = 2
+CHUNKS = 4
 PARTS = 4
 PAIR_VMEM, REDUCE_VMEM = 30, 36
-DEST_BITS, BANK_BITS = 6, 7
+SOURCE_BITS, DEST_BITS, BANK_BITS = 3, 6, 7
+LIVE = 1 << (DEST_BITS + BANK_BITS)
+NEGATIVE = LIVE << 1
+G_AT = DEST_BITS + BANK_BITS + 2
 
 
 def place():
@@ -169,11 +172,10 @@
 
 
 def pair_kernel(
-    dest_ref, source_ref, count_ref, pattern_ref, neg_dest_ref, neg_source_ref, bank_ref, d_ref, g_ref,
-    dp_ref, sp_ref, list_ref, open_ref, gt_v,
+    slot_ref, neg_ref, bank_ref, d_ref, g_ref, dp_ref, sp_ref, list_ref, open_ref, gt_v
 ):
-    stops, cap = dest_ref.shape[2:]
-    neg = neg_dest_ref.shape[2]
+    stops, cap = slot_ref.shape[2:]
+    neg = neg_ref.shape[2]
     sub = sp_ref.shape[0] // stops
     per = dp_ref.shape[0] // stops
     dump = list_ref.shape[0] - 1
@@ -189,13 +191,12 @@
         held = open_ref[src]
         fresh = held < 0
         at = jnp.where(fresh, 2 * pairs, held)
-        list_ref[jnp.where(live, at, dump)] = (code << 2) | 2
+        list_ref[jnp.where(live, at, dump)] = code
         open_ref[src] = jnp.where(live, jnp.where(fresh, 2 * pairs + 1, -1), held)
         return pairs + jnp.where(live & fresh, 1, 0)
 
     def add_stop(stop, pairs):
         group = lax.rem(b - stop + stops, stops) * sub
-        count = count_ref[0, 0, stop]
         for q in range(sub):
             open_ref[q] = -1
             tile = stop * sub + q
@@ -204,16 +205,12 @@
         for q in range(per):
             dp_ref[stop * per + q] = jnp.zeros(dp_ref.shape[1:], dp_ref.dtype)
 
-        def code(src, index, dest, negative):
-            return ((((group + src) << BANK_BITS) | index) << DEST_BITS | dest) << 1 | negative
-
-        for k in range(neg):
-            src = neg_source_ref[0, 0, k, stop]
-            pairs = add_slot(pairs, src, code(src, 0, neg_dest_ref[0, 0, k, stop], 1), True)
-        for k in range(cap):
-            src = source_ref[0, 0, stop, k]
-            value = code(src, pattern_ref[0, 0, stop, k], dest_ref[0, 0, stop, k], 0)
-            pairs = add_slot(pairs, src, value, k < count)
+        for ref, slots in ((neg_ref, neg), (slot_ref, cap)):
+            for k in range(slots):
+                value = ref[0, 0, k, stop] if ref is neg_ref else ref[0, 0, stop, k]
+                src = value & (2**SOURCE_BITS - 1)
+                code = (value >> SOURCE_BITS) | ((group + src) << G_AT)
+                pairs = add_slot(pairs, src, code, (value & (LIVE << SOURCE_BITS)) != 0)
         return pairs
 
     pairs = lax.fori_loop(0, stops, add_stop, 0)
@@ -231,11 +228,11 @@
 
     def first(i):
         codes = [list_ref[2 * i], list_ref[2 * i + 1]]
-        g = codes[0] >> (DEST_BITS + BANK_BITS + 3)
-        p = [(code >> 3) & (2**DEST_BITS - 1) for code in codes]
-        ids = [(code >> (DEST_BITS + 3)) & (2**BANK_BITS - 1) for code in codes]
-        keep = [((code >> 2) & 1) - 1 for code in codes]
-        live = [((code >> 1) & 1).astype(jnp.float32) for code in codes]
+        g = codes[0] >> G_AT
+        p = [code & (2**DEST_BITS - 1) for code in codes]
+        ids = [(code >> DEST_BITS) & (2**BANK_BITS - 1) for code in codes]
+        keep = [((code >> (DEST_BITS + BANK_BITS + 1)) & 1) - 1 for code in codes]
+        live = [((code >> (DEST_BITS + BANK_BITS)) & 1).astype(jnp.float32) for code in codes]
         zq = g_ref[pl.ds(pl.multiple_of(g * T, T), T), :]
         zp = jnp.concatenate([d_ref[pl.ds(pl.multiple_of(k * T, T), T), :] for k in p], axis=0)
         s = lax.dot_general(zq, zp, (((1,), (1,)), ((), ())), preferred_element_type=jnp.float32)
@@ -260,12 +257,12 @@
     lax.fori_loop(0, (pairs + UNROLL - 1) // UNROLL, body, 0)
 
 
-def pair_sums(dest, source, count, pattern, neg_dest, neg_source, bank, d, g):
+def pair_sums(slots, negatives, bank, d, g):
     nd, ng = d.shape[0] // T, g.shape[0] // T
     width = d.shape[1]
-    stops, cap = dest.shape[2:]
+    stops, cap = slots.shape[2:]
     sub = ng // stops
-    most = stops * ((cap + neg_dest.shape[2] + sub) // 2) + UNROLL
+    most = stops * ((cap + negatives.shape[2] + sub) // 2) + UNROLL
     most += (-most) % 8 + 8
     smem = pl.BlockSpec(memory_space=pltpu.SMEM)
     vmem = pl.BlockSpec(memory_space=pltpu.VMEM)
@@ -275,7 +272,7 @@
             jax.ShapeDtypeStruct((nd, width, T), jnp.float32),
             jax.ShapeDtypeStruct((ng, T, width), jnp.float32),
         ),
-        in_specs=[smem] * 6 + [vmem] * 3,
+        in_specs=[smem] * 2 + [vmem] * 3,
         out_specs=(vmem, vmem),
         scratch_shapes=[
             pltpu.SMEM((2 * most,), jnp.int32),
@@ -283,7 +280,7 @@
             pltpu.VMEM((ng, width, T), jnp.bfloat16),
         ],
         compiler_params=pltpu.CompilerParams(vmem_limit_bytes=PAIR_VMEM << 20),
-    )(dest, source, count, pattern, neg_dest, neg_source, bank, d, g)
+    )(slots, negatives, bank, d, g)
 
 
 def code16(value_at, blocks, dst, amax):
@@ -464,17 +461,10 @@
 ):
     rows = embedding.shape[0]
     d, g = gather(embedding)
-    dp, sp = pair_sums(
-        tile_dest,
-        tile_source,
-        tile_count,
-        pattern_id,
-        negative_dest.swapaxes(2, 3),
-        negative_source.swapaxes(2, 3),
-        pattern_bank,
-        d,
-        g,
-    )
+    live = jnp.arange(tile_dest.shape[3], dtype=jnp.int32) < tile_count[..., None]
+    slots = ((pattern_id << DEST_BITS | tile_dest | jnp.where(live, LIVE, 0)) << SOURCE_BITS) | tile_source
+    negatives = ((negative_dest | LIVE | NEGATIVE) << SOURCE_BITS) | negative_source
+    dp, sp = pair_sums(slots, negatives.swapaxes(2, 3), pattern_bank, d, g)
     scale = 1.0 / math.sqrt(T * tile_dest.shape[2])
     return reduce_sums(dp, sp, rows, scale)
 

time: 99.2 us -> 95.3 us (0.961)
  local copies, waits for them, and re-layouts: 6.75 us -> 2.65 us
  other arithmetic: 0 us -> 1.51 us
  Pallas kernels: 92.1 us -> 90.6 us
    unnamed x17 -> x5, local copies, waits for them, and re-layouts: 6.75 us -> 2.65 us
    pallas_call x1, Pallas kernels: 42.4 us -> 41.2 us  [reduce_sums(): pl.pallas_call(functools.partial(reduce_kernel, scale), out_shape=jax.Sha...]
where the time goes in v4:
time: 95.3 us; the launch traced here: 94.8 us
  Pallas kernels  90.6 us (95%)
  local copies, waits for them, and re-layouts  2.65 us (3%)
  other arithmetic  1.51 us (2%)
    pallas_call x1, Pallas kernels, reduce_sums(): pl.pallas_call(functools.partial(reduce_kernel, scale), out_shape=jax.Sha...  41.2 us
    pallas_call x1, Pallas kernels, gather(): pl.pallas_call(gather_kernel, out_shape=(jax.ShapeDtypeStruct((XS * YS *...  29.4 us
    pallas_call x1, Pallas kernels, pair_sums(): pl.pallas_call(pair_kernel, out_shape=(jax.ShapeDtypeStruct((nd, width, T...  20 us
    unnamed x5, local copies, waits for them, and re-layouts  2.65 us

profile of v4, /device:TPU:1, one launch (start us, length us, event | category | flops | bytes accessed | tf_op | source)
XLA Modules:
  0.0 94.8 jit_solution(14044097076026786041)
XLA Ops:
  0.0 0.7 or_bitcast_fusion.neg_ref
  0.7 0.8 shift-left_or_fusion.slot_ref
  1.5 0.0 copy-start
  1.5 0.9 %copy-done = bf16[512,256]{1,0:T(8,128)(2,1)S(1)} copy-done((bf16[512,256]{1,0:T(8,128)(2,1)S(1)}, bf16[512,256]{1,0:T(8,128)(2,1)}, u32[]{:S(2)}) %copy-start) | copy-done | bytes 262168
  2.5 29.4 %shard_map.85 = (bf16[4096,256]{1,0:T(8,128)(2,1)S(1)}, bf16[8192,256]{1,0:T(8,128)(2,1)S(1)}) custom-call(bf16[512,256]{1,0:T(8,128)(2,1)S(1)} %copy-done), custom_call_target="tpu_custom_call" | custom-call | tf_op jit(solution)/shard_map/pallas_call | solution.py:155
  31.9 0.0 copy-start.1
  31.9 0.9 copy-done.1
  32.8 20.0 %shard_map.86 = (f32[32,256,128]{2,1,0:T(8,128)S(1)}, f32[64,128,256]{2,1,0:T(8,128)S(1)}) custom-call(s32[1,1,16,24]{3,2,1,0:T(8,128)S(1)} %shift-left_or_fusion.slot_ref, s32[1,1,4,16]{3,2,1,0:T(4,128)S(1)} %or_bitcast_fusion.neg_ref, s32[64,4,128]{2,1,0:T(4,128)S(1)} %copy-done.1, bf16[4096,256]{1,0:T(8,128)(2,1)S(1)} %get-tuple-element.9.d_ref, ...), custom_call_target="tpu_custom_call" | custom-call | tf_op jit(solution)/shard_map/pallas_call | solution.py:269
  52.8 41.2 %shard_map.87 = f32[512,256]{1,0:T(8,128)S(1)} custom-call(f32[32,256,128]{2,1,0:T(8,128)S(1)} %get-tuple-element.11.dp_ref, f32[64,128,256]{2,1,0:T(8,128)S(1)} %get-tuple-element.12.sp_ref), custom_call_target="tpu_custom_call" | custom-call | tf_op jit(solution)/shard_map/pallas_call | solution.py:438
  94.0 0.8 copy.10
Async XLA Ops:
  1.5 1.0 %copy-start = (bf16[512,256]{1,0:T(8,128)(2,1)S(1)}, bf16[512,256]{1,0:T(8,128)(2,1)}, u32[]{:S(2)}) copy-start(bf16[512,256]{1,0:T(8,128)(2,1)} %e_ref.1) | copy-start | bytes 786436
  31.9 0.9 copy-start.1

commit v5 on v4

--- a/solution.py
+++ b/solution.py
@@ -14,7 +14,7 @@
 UNROLL = 6
 CHUNKS = 4
 PARTS = 4
-PAIR_VMEM, REDUCE_VMEM = 30, 36
+GATHER_VMEM, PAIR_VMEM, REDUCE_VMEM = 14, 28, 36
 SOURCE_BITS, DEST_BITS, BANK_BITS = 3, 6, 7
 LIVE = 1 << (DEST_BITS + BANK_BITS)
 NEGATIVE = LIVE << 1
@@ -55,7 +55,59 @@
     pl.semaphore_wait(barrier, len(to))
 
 
-def gather_kernel(e_ref, d_ref, g_ref, send, recv, local):
+def pair_words(words, block, stops, sub, room):
+    slots, lanes = words.shape
+    f32, bf16 = jnp.float32, jnp.bfloat16
+    lane = lax.broadcasted_iota(jnp.int32, words.shape, 1)
+    src = words & (2**SOURCE_BITS - 1)
+    live = (words & (LIVE << SOURCE_BITS)) != 0
+    picks = [jnp.where(live & (src == q), 1.0, 0.0) for q in range(sub)]
+
+    def earlier(n, axis):
+        shape = (n, n)
+        return jnp.where(
+            lax.broadcasted_iota(jnp.int32, shape, 1 - axis) < lax.broadcasted_iota(jnp.int32, shape, axis), 1.0, 0.0
+        ).astype(bf16)
+
+    before = earlier(slots, 0)
+    ranks = [jnp.dot(before, pick.astype(bf16), preferred_element_type=f32) for pick in picks]
+    held = [(jnp.sum(pick, axis=0, keepdims=True).astype(jnp.int32) + 1 >> 1).astype(f32) for pick in picks]
+    in_stop = functools.reduce(lambda a, b: a + b, held)
+    start = jnp.dot(
+        jnp.broadcast_to(in_stop, (8, lanes)).astype(bf16), earlier(lanes, 1), preferred_element_type=f32
+    )[:1]
+    at = jnp.full(words.shape, -1.0, f32)
+    for q in range(sub):
+        at = jnp.where(picks[q] > 0.0, 2.0 * start + ranks[q], at)
+        start = start + held[q]
+    origin = block - lane
+    origin = jnp.where(origin < 0, origin + stops, origin)
+    code = (words >> SOURCE_BITS) | ((origin * sub + src) << G_AT)
+    code = jnp.where(live, code, 0)
+
+    def turned(values):
+        tall = jnp.concatenate([values, jnp.zeros((lanes - slots, lanes), f32)], axis=0)
+        return tall.T
+
+    bytes_of = [turned(((code >> shift) & 255).astype(f32)) for shift in (0, 8, 16)]
+    row = lax.broadcasted_iota(jnp.int32, (8, lanes), 0)
+    spots = lax.broadcasted_iota(jnp.int32, (slots, room), 1).astype(f32)
+    placed = jnp.zeros((8, room), f32)
+    for stop in range(stops):
+        parts = jnp.zeros((8, lanes), f32)
+        for k in range(3):
+            parts = jnp.where(row == k, jnp.broadcast_to(bytes_of[k][stop : stop + 1], (8, lanes)), parts)
+        hit = jnp.where(jnp.broadcast_to(at[:, stop : stop + 1], spots.shape) == spots, 1.0, 0.0)
+        placed = placed + jnp.dot(
+            parts[:, :slots].astype(bf16), hit.astype(bf16), preferred_element_type=f32
+        )
+    placed = placed.astype(jnp.int32)
+    listed = placed[0:1] | (placed[1:2] << 8) | (placed[2:3] << 16)
+    total = jnp.sum(jnp.where(lane[:1] < stops, in_stop, 0.0), axis=1, keepdims=True).astype(jnp.int32)
+    return jnp.where(lax.broadcasted_iota(jnp.int32, (1, room), 1) == room - 1, total, listed)
+
+
+def gather_kernel(e_ref, slot_ref, neg_ref, d_ref, g_ref, gt_ref, list_ref, words, send, recv, local):
     rows = e_ref.shape[0]
     part = rows // PARTS
     z, xh, c, xl, y = place()
@@ -92,9 +144,21 @@
     def pass_d(name, xx, yy, h, peer):
         push((name, h), d_at(xx, yy, h), d_at(xx, yy, h), peer)
 
+    def turn(block, from_ref=None):
+        def one(i, carry):
+            at = pl.ds(pl.multiple_of((0 if from_ref is not None else block * rows) + i * T, T), T)
+            gt_ref[block * (rows // T) + i] = (g_ref if from_ref is None else from_ref)[at, :].T
+            return carry
+
+        lax.fori_loop(0, rows // T, one, 0)
+
+    shared = []
+
     def share(zz, xx, src=None):
         whole = g_ref.at[pl.ds(blk_of(zz, xx, c) * rows, rows)]
         push(("sib", len(copies)), whole if src is None else src, whole, "sib")
+        shared.append((copies["sib", len(copies) - 1], blk_of(zz, xx, 1 - c)))
+        turn(blk_of(zz, xx, c), src)
 
     keep_d = pltpu.make_async_copy(e_ref, d_ref.at[pl.ds(fiber_of(xl, y) * rows, rows)], local.at[0])
     keep_g = pltpu.make_async_copy(e_ref, g_ref.at[pl.ds(blk_of(z, xh, c) * rows, rows)], local.at[1])
@@ -108,6 +172,19 @@
         push(("y+", h), e_at(h), d_at(xl, y, h), "y+")
         push(("z-", h), e_at(h), g_at(z, xh, h), "z-")
         push(("y-", h), e_at(h), d_at(xl, y, h), "y-")
+
+    share(z, xh, e_ref)
+    stops, cap = slot_ref.shape[2:]
+    neg = neg_ref.shape[2]
+    words[...] = jnp.zeros_like(words)
+    words[0:stops, 0:cap] = slot_ref[0, 0]
+    by_slot = words[...].T
+    words[...] = jnp.zeros_like(words)
+    words[0:cap, :] = by_slot[0:cap]
+    words[cap : cap + neg, 0:stops] = neg_ref[0, 0]
+    list_ref[...] = pair_words(
+        words[0 : cap + neg + 4, :], lax.axis_index("blk"), stops, gt_ref.shape[0] // stops, list_ref.shape[1]
+    )
 
     def second_hop(h):
         got("xl-", h)
@@ -128,7 +205,6 @@
         pass_g("xh+", z, 1 - xh, h, "z+")
         if h:
             second_hop(h - 1)
-    share(z, xh, e_ref)
     share(z + 3, xh)
     share(z, 1 - xh)
     second_hop(PARTS - 1)
@@ -140,80 +216,54 @@
     for h in range(PARTS):
         for name in ("y-", "xl+", "y++", "xl--"):
             got(name, h)
-    for (name, _), copy in copies.items():
-        if name == "sib":
-            copy.wait_recv()
+    for copy, block in shared:
+        copy.wait_recv()
+        turn(block)
     for copy in copies.values():
         copy.wait_send()
     keep_d.wait()
     keep_g.wait()
 
 
-def gather(e):
+def gather(e, slots, negatives):
     rows, width = e.shape
     copies = 14 * PARTS + 8
+    stops, cap = slots.shape[2:]
+    total = ZS * XS * 2 * rows
+    room = stops * (cap + negatives.shape[2] + total // T // stops) + 2 * UNROLL + 1
+    room += (-room) % T
+    vmem, anywhere = pl.BlockSpec(memory_space=pltpu.VMEM), pl.BlockSpec(memory_space=pl.ANY)
     return pl.pallas_call(
         gather_kernel,
         out_shape=(
             jax.ShapeDtypeStruct((XS * YS * rows, width), e.dtype),
-            jax.ShapeDtypeStruct((ZS * XS * 2 * rows, width), e.dtype),
+            jax.ShapeDtypeStruct((total, width), e.dtype),
+            jax.ShapeDtypeStruct((total // T, width, T), e.dtype),
+            jax.ShapeDtypeStruct((1, room), jnp.int32),
         ),
-        in_specs=[pl.BlockSpec(memory_space=pl.ANY)],
-        out_specs=(pl.BlockSpec(memory_space=pl.ANY),) * 2,
+        in_specs=[vmem, vmem, vmem],
+        out_specs=(anywhere, vmem, vmem, vmem),
         scratch_shapes=[
+            pltpu.VMEM((T, T), jnp.int32),
             pltpu.SemaphoreType.DMA((copies,)),
             pltpu.SemaphoreType.DMA((copies,)),
             pltpu.SemaphoreType.DMA((2,)),
         ],
         compiler_params=pltpu.CompilerParams(
-            collective_id=0, has_side_effects=True, vmem_limit_bytes=4 << 20
+            collective_id=0, has_side_effects=True, vmem_limit_bytes=GATHER_VMEM << 20
         ),
-    )(e)
-
-
-def pair_kernel(
-    slot_ref, neg_ref, bank_ref, d_ref, g_ref, dp_ref, sp_ref, list_ref, open_ref, gt_v
-):
-    stops, cap = slot_ref.shape[2:]
-    neg = neg_ref.shape[2]
-    sub = sp_ref.shape[0] // stops
-    per = dp_ref.shape[0] // stops
-    dump = list_ref.shape[0] - 1
-    b = lax.axis_index("blk")
-
-    def preset(i, carry):
-        list_ref[i] = 0
+    )(e, slots, negatives)
+
+
+def pair_kernel(list_ref, bank_ref, d_ref, g_ref, gt_ref, dp_ref, sp_ref):
+    def clear(i, carry):
+        dp_ref[i] = jnp.zeros(dp_ref.shape[1:], dp_ref.dtype)
+        for k in range(sp_ref.shape[0] // dp_ref.shape[0]):
+            sp_ref[i * (sp_ref.shape[0] // dp_ref.shape[0]) + k] = jnp.zeros(sp_ref.shape[1:], sp_ref.dtype)
         return carry
 
-    lax.fori_loop(0, list_ref.shape[0], preset, 0, unroll=16)
-
-    def add_slot(pairs, src, code, live):
-        held = open_ref[src]
-        fresh = held < 0
-        at = jnp.where(fresh, 2 * pairs, held)
-        list_ref[jnp.where(live, at, dump)] = code
-        open_ref[src] = jnp.where(live, jnp.where(fresh, 2 * pairs + 1, -1), held)
-        return pairs + jnp.where(live & fresh, 1, 0)
-
-    def add_stop(stop, pairs):
-        group = lax.rem(b - stop + stops, stops) * sub
-        for q in range(sub):
-            open_ref[q] = -1
-            tile = stop * sub + q
-            gt_v[tile] = g_ref[pl.ds(pl.multiple_of(tile * T, T), T), :].T
-            sp_ref[tile] = jnp.zeros(sp_ref.shape[1:], sp_ref.dtype)
-        for q in range(per):
-            dp_ref[stop * per + q] = jnp.zeros(dp_ref.shape[1:], dp_ref.dtype)
-
-        for ref, slots in ((neg_ref, neg), (slot_ref, cap)):
-            for k in range(slots):
-                value = ref[0, 0, k, stop] if ref is neg_ref else ref[0, 0, stop, k]
-                src = value & (2**SOURCE_BITS - 1)
-                code = (value >> SOURCE_BITS) | ((group + src) << G_AT)
-                pairs = add_slot(pairs, src, code, (value & (LIVE << SOURCE_BITS)) != 0)
-        return pairs
-
-    pairs = lax.fori_loop(0, stops, add_stop, 0)
+    lax.fori_loop(0, dp_ref.shape[0], clear, 0)
+    pairs = list_ref[0, list_ref.shape[1] - 1]
     one_bit = jnp.left_shift(1, lax.broadcasted_iota(jnp.int32, (32, T), 0))
 
     def mask_less_half(index, keep):
@@ -227,7 +277,7 @@
         )
 
     def first(i):
-        codes = [list_ref[2 * i], list_ref[2 * i + 1]]
+        codes = [list_ref[0, 2 * i], list_ref[0, 2 * i + 1]]
         g = codes[0] >> G_AT
         p = [code & (2**DEST_BITS - 1) for code in codes]
         ids = [(code >> DEST_BITS) & (2**BANK_BITS - 1) for code in codes]
@@ -244,7 +294,7 @@
 
     def second(g, p, zp, r):
         to_source = jnp.dot(r, zp, preferred_element_type=jnp.float32)
-        to_dest = jnp.dot(gt_v[g], r, preferred_element_type=jnp.float32)
+        to_dest = jnp.dot(gt_ref[g], r, preferred_element_type=jnp.float32)
         sp_ref[g] += to_source
         dp_ref[p[0]] += to_dest[:, :T]
         dp_ref[p[1]] += to_dest[:, T:]
@@ -257,30 +307,20 @@
     lax.fori_loop(0, (pairs + UNROLL - 1) // UNROLL, body, 0)
 
 
-def pair_sums(slots, negatives, bank, d, g):
-    nd, ng = d.shape[0] // T, g.shape[0] // T
+def pair_sums(words, bank, d, g, gt):
     width = d.shape[1]
-    stops, cap = slots.shape[2:]
-    sub = ng // stops
-    most = stops * ((cap + negatives.shape[2] + sub) // 2) + UNROLL
-    most += (-most) % 8 + 8
     smem = pl.BlockSpec(memory_space=pltpu.SMEM)
     vmem = pl.BlockSpec(memory_space=pltpu.VMEM)
     return pl.pallas_call(
         pair_kernel,
         out_shape=(
-            jax.ShapeDtypeStruct((nd, width, T), jnp.float32),
-            jax.ShapeDtypeStruct((ng, T, width), jnp.float32),
+            jax.ShapeDtypeStruct((d.shape[0] // T, width, T), jnp.float32),
+            jax.ShapeDtypeStruct((g.shape[0] // T, T, width), jnp.float32),
         ),
-        in_specs=[smem] * 2 + [vmem] * 3,
+        in_specs=[smem] + [vmem] * 4,
         out_specs=(vmem, vmem),
-        scratch_shapes=[
-            pltpu.SMEM((2 * most,), jnp.int32),
-            pltpu.SMEM((sub,), jnp.int32),
-            pltpu.VMEM((ng, width, T), jnp.bfloat16),
-        ],
         compiler_params=pltpu.CompilerParams(vmem_limit_bytes=PAIR_VMEM << 20),
-    )(slots, negatives, bank, d, g)
+    )(words, bank, d, g, gt)
 
 
 def code16(value_at, blocks, dst, amax):
@@ -460,11 +500,11 @@
     embedding, tile_dest, tile_source, tile_count, pattern_id, pattern_bank, negative_dest, negative_source
 ):
     rows = embedding.shape[0]
-    d, g = gather(embedding)
     live = jnp.arange(tile_dest.shape[3], dtype=jnp.int32) < tile_count[..., None]
     slots = ((pattern_id << DEST_BITS | tile_dest | jnp.where(live, LIVE, 0)) << SOURCE_BITS) | tile_source
     negatives = ((negative_dest | LIVE | NEGATIVE) << SOURCE_BITS) | negative_source
-    dp, sp = pair_sums(slots, negatives.swapaxes(2, 3), pattern_bank, d, g)
+    d, g, gt, words = gather(embedding, slots, negatives.swapaxes(2, 3))
+    dp, sp = pair_sums(words, pattern_bank, d, g, gt)
     scale = 1.0 / math.sqrt(T * tile_dest.shape[2])
     return reduce_sums(dp, sp, rows, scale)
 

time: 95.3 us -> 91.6 us (0.961)
  Pallas kernels: 90.6 us -> 86.8 us
    pallas_call x1, Pallas kernels: 20 us -> 17 us  [pair_sums(): pl.pallas_call(pair_kernel, out_shape=(jax.ShapeDtypeStruct((d.shape[0] /...]
    pallas_call x1, Pallas kernels: 41.2 us -> 40.2 us  [reduce_sums(): pl.pallas_call(functools.partial(reduce_kernel, scale), out_shape=jax.Sha...]
where the time goes in v5:
time: 91.6 us; the launch traced here: 91 us
  Pallas kernels  86.8 us (95%)
  local copies, waits for them, and re-layouts  2.65 us (3%)
  other arithmetic  1.51 us (2%)
    pallas_call x1, Pallas kernels, reduce_sums(): pl.pallas_call(functools.partial(reduce_kernel, scale), out_shape=jax.Sha...  40.2 us
    pallas_call x1, Pallas kernels, gather(): pl.pallas_call(gather_kernel, out_shape=(jax.ShapeDtypeStruct((XS * YS *...  29.7 us
    pallas_call x1, Pallas kernels, pair_sums(): pl.pallas_call(pair_kernel, out_shape=(jax.ShapeDtypeStruct((d.shape[0] /...  17 us
    unnamed x5, local copies, waits for them, and re-layouts  2.65 us

profile of v5, /device:TPU:1, one launch (start us, length us, event | category | flops | bytes accessed | tf_op | source)
XLA Modules:
  0.0 91.0 jit_solution(1161457233831000708)
XLA Ops:
  0.0 0.7 or_bitcast_fusion.neg_ref
  0.7 0.8 shift-left_or_fusion.slot_ref
  1.5 0.0 copy-start
  1.5 0.9 %copy-done = bf16[512,256]{1,0:T(8,128)(2,1)S(1)} copy-done((bf16[512,256]{1,0:T(8,128)(2,1)S(1)}, bf16[512,256]{1,0:T(8,128)(2,1)}, u32[]{:S(2)}) %copy-start) | copy-done | bytes 262168
  2.5 29.7 %shard_map.85 = (bf16[4096,256]{1,0:T(8,128)(2,1)S(1)}, bf16[8192,256]{1,0:T(8,128)(2,1)S(1)}, bf16[64,256,128]{2,1,0:T(8,128)(2,1)S(1)}, s32[1,640]{1,0:T(1,128)S(1)}) custom-call(bf16[512,256]{1,0:T(8,128)(2,1)S(1)} %copy-done, s32[1,1,16,24]{3,2,1,0:T(8,128)S(1)} %shift-left_or_fusion.slot_ref, s32[1,1,4,16]{3,2,1,0:T(4,128)S(1)} %or_bitcast_fusion.neg_ref), custom_call_target="tpu_custom_call" | custom-call | tf_op jit(solution)/shard_map/pallas_call | solution.py:236
  32.2 0.0 copy-start.1
  32.2 0.9 copy-done.1
  33.1 17.0 %shard_map.86 = (f32[32,256,128]{2,1,0:T(8,128)S(1)}, f32[64,128,256]{2,1,0:T(8,128)S(1)}) custom-call(s32[1,640]{1,0:T(1,128)S(1)} %get-tuple-element.11.list_ref, s32[64,4,128]{2,1,0:T(4,128)S(1)} %copy-done.1, bf16[4096,256]{1,0:T(8,128)(2,1)S(1)} %get-tuple-element.12.d_ref, bf16[8192,256]{1,0:T(8,128)(2,1)S(1)} %get-tuple-element.13.g_ref, ...), custom_call_target="tpu_custom_call" | custom-call | tf_op jit(solution)/shard_map/pallas_call | solution.py:314
  50.0 40.2 %shard_map.87 = f32[512,256]{1,0:T(8,128)S(1)} custom-call(f32[32,256,128]{2,1,0:T(8,128)S(1)} %get-tuple-element.15.dp_ref, f32[64,128,256]{2,1,0:T(8,128)S(1)} %get-tuple-element.16.sp_ref), custom_call_target="tpu_custom_call" | custom-call | tf_op jit(solution)/shard_map/pallas_call | solution.py:478
  90.2 0.8 copy.10
Async XLA Ops:
  1.5 1.0 %copy-start = (bf16[512,256]{1,0:T(8,128)(2,1)S(1)}, bf16[512,256]{1,0:T(8,128)(2,1)}, u32[]{:S(2)}) copy-start(bf16[512,256]{1,0:T(8,128)(2,1)} %e_ref.1) | copy-start | bytes 786436
  32.2 0.9 copy-start.1

commit v6 on v5

--- a/solution.py
+++ b/solution.py
@@ -12,7 +12,6 @@
 T = 128
 MESH = pl.DeviceIdType.MESH
 UNROLL = 6
-CHUNKS = 4
 PARTS = 4
 GATHER_VMEM, PAIR_VMEM, REDUCE_VMEM = 14, 28, 36
 SOURCE_BITS, DEST_BITS, BANK_BITS = 3, 6, 7
@@ -323,26 +322,16 @@
     )(words, bank, d, g, gt)
 
 
-def code16(value_at, blocks, dst, amax):
-    height = (dst.shape[0] - 16) // blocks
-    power = jnp.ceil(jnp.log2(jnp.maximum(amax, 1e-37)))
-    gain = jnp.exp2(-power) * 32767.0
-
-    def one(i, carry):
-        q = jnp.clip(jnp.round(value_at(i) * gain), -32767.0, 32767.0)
-        dst[pl.ds(pl.multiple_of(i * height, height), height), :] = q.astype(jnp.int32).astype(jnp.int16)
-        return carry
-
-    lax.fori_loop(0, blocks, one, 0)
-    dst[pl.ds(blocks * height, 16), :] = jnp.broadcast_to(power, (16, power.shape[1])).astype(jnp.int32).astype(jnp.int16)
-
-
-def reduce_kernel(
-    scale, dp_ref, sp_ref, out_ref, dest, core, s_send, s_recv, d_send, d_recv, send, recv
-):
+LEVELS = 32760.0
+HEAD = 16
+
+
+def power_of(bound):
+    return jnp.ceil(jnp.log2(jnp.maximum(bound, 1e-37)))
+
+
+def reduce_kernel(scale, dp_ref, sp_ref, out_ref, core, s_send, s_recv, d_send, d_recv, send, recv):
     sub = core.shape[1]
-    width = core.shape[3]
-    per = sub // CHUNKS
     z, xh, c, xl, y = place()
     to = peers()
     copies = {}
@@ -359,114 +348,123 @@
         )
         copies[name].start()
 
-    def got(name):
-        copies[name].wait_recv()
-
     order = [(2, 0), (2, 1), (1, 1), (3, 0), (1, 0), (3, 1), (0, 0), (0, 1)]
 
     def s_at(n, core_at):
         dz, xx = order[n]
         return sp_ref.at[pl.ds(blk_of(z + dz, xx, core_at) * sub, sub)]
 
-    def mine(n, h):
-        dy, xx = order[n]
-        return plain(dp_ref.at[pl.ds(fiber_of(xx, y + dy) * sub, sub)], h)
+    def d_at(dy, xx):
+        return dp_ref.at[pl.ds(fiber_of(xx, y + dy) * sub, sub)]
+
+    def largest(ref):
+        def one(i, most):
+            return jnp.maximum(most, jnp.max(jnp.abs(ref[i]), axis=0, keepdims=True))
+
+        return lax.fori_loop(0, sub, one, jnp.zeros((1, ref.shape[2]), jnp.float32))
+
+    def sum_cores(n):
+        copies[f"c{n}"].wait_recv()
+        mine, total = s_at(n, c), core.at[n]
+
+        def one(i, most):
+            value = total[i] + mine[i]
+            total[i] = value
+            return jnp.maximum(most, jnp.max(jnp.abs(value), axis=0, keepdims=True))
+
+        return lax.fori_loop(0, sub, one, jnp.zeros((1, core.shape[3]), jnp.float32))
+
+    def span(h, height):
+        return pl.ds(0, HEAD + height) if h == 0 else pl.ds(HEAD + h * height, height)
+
+    def send_tile(name, h, value, power, out_buf, in_buf, peer):
+        height = value.shape[0]
+        q = jnp.round(value * (jnp.exp2(-power) * LEVELS))
+        out_buf[pl.ds(HEAD + h * height, height), :] = q.astype(jnp.int32).astype(jnp.int16)
+        if h == 0:
+            out_buf[pl.ds(0, HEAD), :] = (
+                jnp.broadcast_to(power, (HEAD, power.shape[1])).astype(jnp.int32).astype(jnp.int16)
+            )
+        push(f"{name}{h}", out_buf.at[span(h, height)], in_buf.at[span(h, height)], peer)
+
+    def bound_in(buf):
+        return jnp.exp2(buf[pl.ds(0, HEAD), :].astype(jnp.float32)[:1])
+
+    def tile_in(buf, h, bound):
+        height = (buf.shape[0] - HEAD) // sub
+        return buf[pl.ds(HEAD + h * height, height), :].astype(jnp.float32) * (bound * (1.0 / LEVELS))
+
+    def got(*names):
+        for name in names:
+            copies[name].wait_recv()
+
+    def y_send(k, h, value, power):
+        send_tile(f"y{k}_", h, value, power, d_send.at[k], d_recv.at[k], "y+" if k % 2 == 0 else "y-")
+
+    def z_send(k, h, value, power):
+        send_tile(f"z{k}_", h, value, power, s_send.at[k], s_recv.at[k], "z+" if k % 2 == 0 else "z-")
 
     meet(to)
     for n in range(8):
         push(f"c{n}", s_at(n, 1 - c), core.at[n], "sib")
-
-    def decoded(ref, h, height):
-        gain = jnp.exp2(ref[h, pl.ds(per * height, 16), :].astype(jnp.float32)[:1]) * (1.0 / 32767.0)
-
-        def at(i):
-            rows = pl.ds(pl.multiple_of(i * height, height), height)
-            return ref[h, rows, :].astype(jnp.float32) * gain
-
-        return at
-
-    def plain(ref, h):
-        return lambda i: ref[h * per + i]
-
-    def total(parts, keep, h):
-        def one(i, most):
-            value = parts[0](i)
-            for part in parts[1:]:
-                value = value + part(i)
-            keep[h * per + i] = value
-            return jnp.maximum(most, jnp.max(jnp.abs(value), axis=0, keepdims=True))
-
-        return lax.fori_loop(0, per, one, jnp.zeros((1, keep.shape[2]), jnp.float32))
-
-    def hand_on(name, parts, keep, h, out_buf, in_buf, peer):
-        amax = total(parts, keep, h)
-        code16(plain(keep, h), per, out_buf.at[h], amax)
-        push(name + str(h), out_buf.at[h], in_buf.at[h], peer)
-
-    def z_send(k, h, peer, *parts):
-        hand_on(f"z{k}", parts, core.at[k], h, s_send.at[k], s_recv.at[k], peer)
-
-    def y_send(k, h, peer, *parts):
-        hand_on(f"y{k}", parts, dest.at[k], h, d_send.at[k], d_recv.at[k], peer)
-
-    def s_in(name, k, h):
-        got(name + str(h))
-        return decoded(s_recv.at[k], h, T)
-
-    def d_in(name, k, h):
-        got(name + str(h))
-        return decoded(d_recv.at[k], h, width)
-
-    def cores(n, h):
-        return plain(core.at[n], h), plain(s_at(n, c), h)
-
-    y_send(0, 0, "y+", mine(0, 0))
-    y_send(1, 0, "y-", mine(1, 0))
-    got("c0")
-    z_send(0, 0, "z+", *cores(0, 0))
-    got("c1")
-    z_send(1, 0, "z-", *cores(1, 0))
-    for h in range(1, CHUNKS):
-        y_send(0, h, "y+", mine(0, h))
-        y_send(1, h, "y-", mine(1, h))
-        z_send(0, h, "z+", *cores(0, h))
-        z_send(1, h, "z-", *cores(1, h))
-    for n in range(2, 8):
-        got(f"c{n}")
-    for h in range(CHUNKS):
-        y_send(2, h, "y+", mine(2, h))
-        y_send(3, h, "y-", mine(3, h))
-        z_send(2, h, "z+", *cores(2, h))
-        z_send(3, h, "z-", *cores(3, h))
-        y_send(4, h, "y+", mine(4, h), d_in("y0", 0, h))
-        y_send(5, h, "y-", mine(5, h), d_in("y1", 1, h))
-        z_send(4, h, "z+", *cores(4, h), s_in("z0", 0, h))
-        z_send(5, h, "z-", *cores(5, h), s_in("z1", 1, h))
-    for h in range(CHUNKS):
-        most_d = [
-            total((mine(6, h), d_in("y3", 3, h), d_in("y4", 4, h)), dest.at[6], h),
-            total((mine(7, h), d_in("y2", 2, h), d_in("y5", 5, h)), dest.at[7], h),
-        ]
-        code16(plain(dest.at[7 - xl], h), per, d_send.at[6, h], jnp.where(xl == 0, most_d[1], most_d[0]))
-        push(f"xl{h}", d_send.at[6, h], d_recv.at[6, h], "xl")
-        most_s = [
-            total((*cores(6, h), s_in("z3", 3, h), s_in("z4", 4, h)), core.at[6], h),
-            total((*cores(7, h), s_in("z2", 2, h), s_in("z5", 5, h)), core.at[7], h),
-        ]
-        code16(plain(core.at[7 - xh], h), per, s_send.at[6, h], jnp.where(xh == 0, most_s[1], most_s[0]))
-        push(f"xh{h}", s_send.at[6, h], s_recv.at[6, h], "xh")
-    for h in range(CHUNKS):
-        from_xl = d_in("xl", 6, h)
-        from_xh = s_in("xh", 6, h)
-
-        def finish(i, carry):
-            by_dest = dest[6 + xl, h * per + i] + from_xl(i)
-            by_source = core[6 + xh, h * per + i] + from_xh(i)
-            rows = pl.ds(pl.multiple_of((h * per + i) * T, T), T)
-            out_ref[rows, :] = (by_source + by_dest.T) * scale
-            return carry
-
-        lax.fori_loop(0, per, finish, 0)
+    for k in (0, 1):
+        part = d_at(*order[k])
+        power = power_of(largest(part))
+        for h in range(sub):
+            y_send(k, h, part[h], power)
+    for k in (0, 1):
+        power = power_of(sum_cores(k))
+        for h in range(sub):
+            z_send(k, h, core[k, h], power)
+    most_d = [largest(d_at(*order[k])) for k in (4, 5, 2, 3)]
+    most_s = [sum_cores(k) for k in (4, 5, 2, 3)]
+    own_d, own_s = [power_of(most) for most in most_d[2:]], [power_of(most) for most in most_s[2:]]
+    on_d, on_s, from_d, from_s = [], [], [], []
+    for h in range(sub):
+        for k in (0, 1):
+            got(f"y{k}_{h}")
+            if h == 0:
+                from_d.append(bound_in(d_recv.at[k]))
+                on_d.append(power_of(most_d[k] + from_d[k]))
+            y_send(4 + k, h, d_at(*order[4 + k])[h] + tile_in(d_recv.at[k], h, from_d[k]), on_d[k])
+            y_send(2 + k, h, d_at(*order[2 + k])[h], own_d[k])
+            got(f"z{k}_{h}")
+            if h == 0:
+                from_s.append(bound_in(s_recv.at[k]))
+                on_s.append(power_of(most_s[k] + from_s[k]))
+            z_send(4 + k, h, core[4 + k, h] + tile_in(s_recv.at[k], h, from_s[k]), on_s[k])
+            z_send(2 + k, h, core[2 + k, h], own_s[k])
+    most_6, most_7 = sum_cores(6), sum_cores(7)
+    away_d, away_s = d_at(0, 1 - xl), core.at[7 - xh]
+    most_away_d = largest(away_d)
+    most_away_s = jnp.where(xh == 0, most_7, most_6)
+    for h in range(sub):
+        got(f"y2_{h}", f"y3_{h}", f"y4_{h}", f"y5_{h}")
+        if h == 0:
+            near_d, far_d = bound_in(d_recv.at[2 + xl]), bound_in(d_recv.at[5 - xl])
+            power_d = power_of(most_away_d + near_d + far_d)
+        value = away_d[h] + tile_in(d_recv.at[2 + xl], h, near_d) + tile_in(d_recv.at[5 - xl], h, far_d)
+        send_tile("xl", h, value, power_d, d_send.at[6], d_recv.at[6], "xl")
+        got(f"z2_{h}", f"z3_{h}", f"z4_{h}", f"z5_{h}")
+        if h == 0:
+            near_s, far_s = bound_in(s_recv.at[2 + xh]), bound_in(s_recv.at[5 - xh])
+            power_s = power_of(most_away_s + near_s + far_s)
+        value = away_s[h] + tile_in(s_recv.at[2 + xh], h, near_s) + tile_in(s_recv.at[5 - xh], h, far_s)
+        send_tile("xh", h, value, power_s, s_send.at[6], s_recv.at[6], "xh")
+    home_d, home_s = d_at(0, xl), core.at[6 + xh]
+    bufs_d = [d_recv.at[3 - xl], d_recv.at[4 + xl], d_recv.at[6]]
+    bufs_s = [s_recv.at[3 - xh], s_recv.at[4 + xh], s_recv.at[6]]
+    for h in range(sub):
+        rows = pl.ds(h * T, T)
+        got(f"xl{h}")
+        by_dest = home_d[h]
+        for buf in bufs_d:
+            by_dest = by_dest + tile_in(buf, h, bound_in(buf))
+        got(f"xh{h}")
+        by_source = home_s[h]
+        for buf in bufs_s:
+            by_source = by_source + tile_in(buf, h, bound_in(buf))
+        out_ref[rows, :] = (by_source + by_dest.T) * scale
     for copy in copies.values():
         copy.wait_send()
 
@@ -474,21 +472,20 @@
 def reduce_sums(dp, sp, rows, scale):
     width = sp.shape[2]
     sub = rows // T
-    per = sub // CHUNKS
+    copies = 8 + 14 * sub
     return pl.pallas_call(
         functools.partial(reduce_kernel, scale),
         out_shape=jax.ShapeDtypeStruct((rows, width), jnp.float32),
         in_specs=[pl.BlockSpec(memory_space=pltpu.VMEM)] * 2,
         out_specs=pl.BlockSpec(memory_space=pltpu.VMEM),
         scratch_shapes=[
-            pltpu.VMEM((8, sub, width, T), jnp.float32),
             pltpu.VMEM((8, sub, T, width), jnp.float32),
-            pltpu.VMEM((7, CHUNKS, per * T + 16, width), jnp.int16),
-            pltpu.VMEM((7, CHUNKS, per * T + 16, width), jnp.int16),
-            pltpu.VMEM((7, CHUNKS, per * width + 16, T), jnp.int16),
-            pltpu.VMEM((7, CHUNKS, per * width + 16, T), jnp.int16),
-            pltpu.SemaphoreType.DMA((8 + 14 * CHUNKS,)),
-            pltpu.SemaphoreType.DMA((8 + 14 * CHUNKS,)),
+            pltpu.VMEM((7, HEAD + sub * T, width), jnp.int16),
+            pltpu.VMEM((7, HEAD + sub * T, width), jnp.int16),
+            pltpu.VMEM((7, HEAD + sub * width, T), jnp.int16),
+            pltpu.VMEM((7, HEAD + sub * width, T), jnp.int16),
+            pltpu.SemaphoreType.DMA((copies,)),
+            pltpu.SemaphoreType.DMA((copies,)),
         ],
         compiler_params=pltpu.CompilerParams(
             collective_id=1, has_side_effects=True, vmem_limit_bytes=REDUCE_VMEM << 20

time: 91.6 us -> 92.5 us (level)
  no operation moved by 1% of the time
where the time goes in v6:
time: 92.5 us; the launch traced here: 91.6 us
  Pallas kernels  87.4 us (94%)
  local copies, waits for them, and re-layouts  2.65 us (3%)
  other arithmetic  1.51 us (2%)
    pallas_call x1, Pallas kernels, reduce_sums(): pl.pallas_call(functools.partial(reduce_kernel, scale), out_shape=jax.Sha...  40.8 us
    pallas_call x1, Pallas kernels, gather(): pl.pallas_call(gather_kernel, out_shape=(jax.ShapeDtypeStruct((XS * YS *...  29.7 us
    pallas_call x1, Pallas kernels, pair_sums(): pl.pallas_call(pair_kernel, out_shape=(jax.ShapeDtypeStruct((d.shape[0] /...  17 us
    unnamed x5, local copies, waits for them, and re-layouts  2.65 us

profile of v6, /device:TPU:1, one launch (start us, length us, event | category | flops | bytes accessed | tf_op | source)
XLA Modules:
  0.0 91.6 jit_solution(1093805145496859346)
XLA Ops:
  0.0 0.7 or_bitcast_fusion.neg_ref
  0.7 0.8 shift-left_or_fusion.slot_ref
  1.5 0.0 copy-start
  1.5 0.9 %copy-done = bf16[512,256]{1,0:T(8,128)(2,1)S(1)} copy-done((bf16[512,256]{1,0:T(8,128)(2,1)S(1)}, bf16[512,256]{1,0:T(8,128)(2,1)}, u32[]{:S(2)}) %copy-start) | copy-done | bytes 262168
  2.5 29.7 %shard_map.85 = (bf16[4096,256]{1,0:T(8,128)(2,1)S(1)}, bf16[8192,256]{1,0:T(8,128)(2,1)S(1)}, bf16[64,256,128]{2,1,0:T(8,128)(2,1)S(1)}, s32[1,640]{1,0:T(1,128)S(1)}) custom-call(bf16[512,256]{1,0:T(8,128)(2,1)S(1)} %copy-done, s32[1,1,16,24]{3,2,1,0:T(8,128)S(1)} %shift-left_or_fusion.slot_ref, s32[1,1,4,16]{3,2,1,0:T(4,128)S(1)} %or_bitcast_fusion.neg_ref), custom_call_target="tpu_custom_call" | custom-call | tf_op jit(solution)/shard_map/pallas_call | solution.py:235
  32.2 0.0 copy-start.1
  32.2 0.9 copy-done.1
  33.1 17.0 %shard_map.86 = (f32[32,256,128]{2,1,0:T(8,128)S(1)}, f32[64,128,256]{2,1,0:T(8,128)S(1)}) custom-call(s32[1,640]{1,0:T(1,128)S(1)} %get-tuple-element.11.list_ref, s32[64,4,128]{2,1,0:T(4,128)S(1)} %copy-done.1, bf16[4096,256]{1,0:T(8,128)(2,1)S(1)} %get-tuple-element.12.d_ref, bf16[8192,256]{1,0:T(8,128)(2,1)S(1)} %get-tuple-element.13.g_ref, ...), custom_call_target="tpu_custom_call" | custom-call | tf_op jit(solution)/shard_map/pallas_call | solution.py:313
  50.0 40.8 %shard_map.87 = f32[512,256]{1,0:T(8,128)S(1)} custom-call(f32[32,256,128]{2,1,0:T(8,128)S(1)} %get-tuple-element.15.dp_ref, f32[64,128,256]{2,1,0:T(8,128)S(1)} %get-tuple-element.16.sp_ref), custom_call_target="tpu_custom_call" | custom-call | tf_op jit(solution)/shard_map/pallas_call | solution.py:476
  90.8 0.8 copy.10
Async XLA Ops:
  1.5 1.0 %copy-start = (bf16[512,256]{1,0:T(8,128)(2,1)S(1)}, bf16[512,256]{1,0:T(8,128)(2,1)}, u32[]{:S(2)}) copy-start(bf16[512,256]{1,0:T(8,128)(2,1)} %e_ref.1) | copy-start | bytes 786436
  32.2 0.9 copy-start.1

commit v7 on v6

--- a/solution.py
+++ b/solution.py
@@ -11,7 +11,7 @@
 ZS, XS, YS = 4, 2, 4
 T = 128
 MESH = pl.DeviceIdType.MESH
-UNROLL = 6
+UNROLL = 8
 PARTS = 4
 GATHER_VMEM, PAIR_VMEM, REDUCE_VMEM = 14, 28, 36
 SOURCE_BITS, DEST_BITS, BANK_BITS = 3, 6, 7
@@ -106,7 +106,7 @@
     return jnp.where(lax.broadcasted_iota(jnp.int32, (1, room), 1) == room - 1, total, listed)
 
 
-def gather_kernel(e_ref, slot_ref, neg_ref, d_ref, g_ref, gt_ref, list_ref, words, send, recv, local):
+def gather_kernel(stops, e_ref, slot_ref, d_ref, g_ref, gt_ref, list_ref, words, send, recv, local):
     rows = e_ref.shape[0]
     part = rows // PARTS
     z, xh, c, xl, y = place()
@@ -152,6 +152,12 @@
         lax.fori_loop(0, rows // T, one, 0)
 
     shared = []
+
+    def absorb():
+        copy, block = shared.pop(0)
+        copy.wait_recv()
+        turn(block)
+
 
     def share(zz, xx, src=None):
         whole = g_ref.at[pl.ds(blk_of(zz, xx, c) * rows, rows)]
@@ -173,14 +179,14 @@
         push(("y-", h), e_at(h), d_at(xl, y, h), "y-")
 
     share(z, xh, e_ref)
-    stops, cap = slot_ref.shape[2:]
-    neg = neg_ref.shape[2]
+    cap = slot_ref.shape[3]
+    neg = slot_ref.shape[2] - stops
     words[...] = jnp.zeros_like(words)
-    words[0:stops, 0:cap] = slot_ref[0, 0]
+    words[0:stops, 0:cap] = slot_ref[0, 0, 0:stops]
     by_slot = words[...].T
     words[...] = jnp.zeros_like(words)
     words[0:cap, :] = by_slot[0:cap]
-    words[cap : cap + neg, 0:stops] = neg_ref[0, 0]
+    words[cap : cap + neg, 0:stops] = slot_ref[0, 0, stops : stops + neg, 0:stops]
     list_ref[...] = pair_words(
         words[0 : cap + neg + 4, :], lax.axis_index("blk"), stops, gt_ref.shape[0] // stops, list_ref.shape[1]
     )
@@ -208,39 +214,40 @@
     share(z, 1 - xh)
     second_hop(PARTS - 1)
     share(z + 1, 1 - xh)
+    absorb()
     for name, zz, xx in (("z-", z + 1, xh), ("z++", z + 2, xh), ("xh+", z + 3, 1 - xh), ("xh--", z + 2, 1 - xh)):
         for h in range(PARTS):
             got(name, h)
         share(zz, xx)
+        absorb()
     for h in range(PARTS):
         for name in ("y-", "xl+", "y++", "xl--"):
             got(name, h)
-    for copy, block in shared:
-        copy.wait_recv()
-        turn(block)
+    while shared:
+        absorb()
     for copy in copies.values():
         copy.wait_send()
     keep_d.wait()
     keep_g.wait()
 
 
-def gather(e, slots, negatives):
+def gather(e, slots, stops):
     rows, width = e.shape
     copies = 14 * PARTS + 8
-    stops, cap = slots.shape[2:]
+    cap, neg = slots.shape[3], slots.shape[2] - stops
     total = ZS * XS * 2 * rows
-    room = stops * (cap + negatives.shape[2] + total // T // stops) + 2 * UNROLL + 1
+    room = stops * (cap + neg + total // T // stops) + 4 * UNROLL + 1
     room += (-room) % T
     vmem, anywhere = pl.BlockSpec(memory_space=pltpu.VMEM), pl.BlockSpec(memory_space=pl.ANY)
     return pl.pallas_call(
-        gather_kernel,
+        functools.partial(gather_kernel, stops),
         out_shape=(
             jax.ShapeDtypeStruct((XS * YS * rows, width), e.dtype),
             jax.ShapeDtypeStruct((total, width), e.dtype),
             jax.ShapeDtypeStruct((total // T, width, T), e.dtype),
             jax.ShapeDtypeStruct((1, room), jnp.int32),
         ),
-        in_specs=[vmem, vmem, vmem],
+        in_specs=[vmem, vmem],
         out_specs=(anywhere, vmem, vmem, vmem),
         scratch_shapes=[
             pltpu.VMEM((T, T), jnp.int32),
@@ -251,10 +258,10 @@
         compiler_params=pltpu.CompilerParams(
             collective_id=0, has_side_effects=True, vmem_limit_bytes=GATHER_VMEM << 20
         ),
-    )(e, slots, negatives)
-
-
-def pair_kernel(list_ref, bank_ref, d_ref, g_ref, gt_ref, dp_ref, sp_ref):
+    )(e, slots)
+
+
+def pair_kernel(list_ref, bank_ref, d_ref, g_ref, gt_ref, dp_ref, sp_ref, coded):
     def clear(i, carry):
         dp_ref[i] = jnp.zeros(dp_ref.shape[1:], dp_ref.dtype)
         for k in range(sp_ref.shape[0] // dp_ref.shape[0]):
@@ -275,32 +282,45 @@
             axis=0,
         )
 
+    def tiles(i):
+        codes = [list_ref[0, 2 * i], list_ref[0, 2 * i + 1]]
+        p = [code & (2**DEST_BITS - 1) for code in codes]
+        zp = jnp.concatenate([d_ref[pl.ds(pl.multiple_of(k * T, T), T), :] for k in p], axis=0)
+        return codes[0] >> G_AT, p, zp
+
     def first(i):
         codes = [list_ref[0, 2 * i], list_ref[0, 2 * i + 1]]
-        g = codes[0] >> G_AT
-        p = [code & (2**DEST_BITS - 1) for code in codes]
+        g, _, zp = tiles(i)
         ids = [(code >> DEST_BITS) & (2**BANK_BITS - 1) for code in codes]
         keep = [((code >> (DEST_BITS + BANK_BITS + 1)) & 1) - 1 for code in codes]
         live = [((code >> (DEST_BITS + BANK_BITS)) & 1).astype(jnp.float32) for code in codes]
         zq = g_ref[pl.ds(pl.multiple_of(g * T, T), T), :]
-        zp = jnp.concatenate([d_ref[pl.ds(pl.multiple_of(k * T, T), T), :] for k in p], axis=0)
         s = lax.dot_general(zq, zp, (((1,), (1,)), ((), ())), preferred_element_type=jnp.float32)
         half = 0.5 * jnp.tanh(0.5 * s)
         r = jnp.concatenate(
             [live[u] * (mask_less_half(ids[u], keep[u]) - half[:, u * T : (u + 1) * T]) for u in range(2)], axis=1
         ).astype(jnp.bfloat16)
-        return g, p, zp, r
-
-    def second(g, p, zp, r):
+        return r
+
+    def second(i, r):
+        g, p, zp = tiles(i)
         to_source = jnp.dot(r, zp, preferred_element_type=jnp.float32)
         to_dest = jnp.dot(gt_ref[g], r, preferred_element_type=jnp.float32)
         sp_ref[g] += to_source
         dp_ref[p[0]] += to_dest[:, :T]
         dp_ref[p[1]] += to_dest[:, T:]
 
+    for u in range(UNROLL):
+        coded[0, u] = first(u)
+
     def body(step, carry):
-        for held in [first(step * UNROLL + u) for u in range(UNROLL)]:
-            second(*held)
+        now = lax.rem(step, 2)
+        later = []
+        for u in range(UNROLL):
+            later.append(first((step + 1) * UNROLL + u))
+            second(step * UNROLL + u, coded[now, u])
+        for u in range(UNROLL):
+            coded[1 - now, u] = later[u]
         return carry
 
     lax.fori_loop(0, (pairs + UNROLL - 1) // UNROLL, body, 0)
@@ -318,6 +338,7 @@
         ),
         in_specs=[smem] + [vmem] * 4,
         out_specs=(vmem, vmem),
+        scratch_shapes=[pltpu.VMEM((2, UNROLL, T, 2 * T), d.dtype)],
         compiler_params=pltpu.CompilerParams(vmem_limit_bytes=PAIR_VMEM << 20),
     )(words, bank, d, g, gt)
 
@@ -500,7 +521,9 @@
     live = jnp.arange(tile_dest.shape[3], dtype=jnp.int32) < tile_count[..., None]
     slots = ((pattern_id << DEST_BITS | tile_dest | jnp.where(live, LIVE, 0)) << SOURCE_BITS) | tile_source
     negatives = ((negative_dest | LIVE | NEGATIVE) << SOURCE_BITS) | negative_source
-    d, g, gt, words = gather(embedding, slots, negatives.swapaxes(2, 3))
+    negatives = negatives.swapaxes(2, 3)
+    wide = jnp.pad(negatives, ((0, 0), (0, 0), (0, 0), (0, slots.shape[3] - negatives.shape[3])))
+    d, g, gt, words = gather(embedding, jnp.concatenate([slots, wide], axis=2), tile_dest.shape[2])
     dp, sp = pair_sums(words, pattern_bank, d, g, gt)
     scale = 1.0 / math.sqrt(T * tile_dest.shape[2])
     return reduce_sums(dp, sp, rows, scale)

time: 92.5 us -> 87.8 us (0.949)
  Pallas kernels: 87.4 us -> 83.3 us
    pallas_call x1, Pallas kernels: 40.8 us -> 33.8 us  [reduce_sums(): pl.pallas_call(functools.partial(reduce_kernel, scale), out_shape=jax.Sha...]
    pallas_call x1, Pallas kernels: 17 us -> 19.9 us  [pair_sums(): pl.pallas_call(pair_kernel, out_shape=(jax.ShapeDtypeStruct((d.shape[0] /...]
where the time goes in v7:
time: 87.8 us; the launch traced here: 87.5 us
  Pallas kernels  83.3 us (95%)
  local copies, waits for them, and re-layouts  2.64 us (3%)
  other arithmetic  1.52 us (2%)
    pallas_call x1, Pallas kernels, reduce_sums(): pl.pallas_call(functools.partial(reduce_kernel, scale), out_shape=jax.Sha...  33.8 us
    pallas_call x1, Pallas kernels, gather(): pl.pallas_call(functools.partial(gather_kernel, stops), out_shape=(jax.Sh...  29.7 us
    pallas_call x1, Pallas kernels, pair_sums(): pl.pallas_call(pair_kernel, out_shape=(jax.ShapeDtypeStruct((d.shape[0] /...  19.9 us
    unnamed x5, local copies, waits for them, and re-layouts  2.64 us

profile of v7, /device:TPU:1, one launch (start us, length us, event | category | flops | bytes accessed | tf_op | source)
XLA Modules:
  0.0 87.5 jit_solution(8362935665749563772)
XLA Ops:
  0.0 0.7 or_bitcast_fusion
  0.7 0.8 shift-left_or_fusion
  1.5 0.0 copy-start
  1.5 0.9 %copy-done = bf16[512,256]{1,0:T(8,128)(2,1)S(1)} copy-done((bf16[512,256]{1,0:T(8,128)(2,1)S(1)}, bf16[512,256]{1,0:T(8,128)(2,1)}, u32[]{:S(2)}) %copy-start) | copy-done | bytes 262168
  2.5 29.7 %shard_map.85 = (bf16[4096,256]{1,0:T(8,128)(2,1)S(1)}, bf16[8192,256]{1,0:T(8,128)(2,1)S(1)}, bf16[64,256,128]{2,1,0:T(8,128)(2,1)S(1)}, s32[1,640]{1,0:T(1,128)S(1)}) custom-call(bf16[512,256]{1,0:T(8,128)(2,1)S(1)} %copy-done, s32[1,1,20,24]{3,2,1,0:T(8,128)S(1)} %pad_add_fusion.slot_ref), custom_call_target="tpu_custom_call" | custom-call | tf_op jit(solution)/shard_map/pallas_call | solution.py:242
  32.2 0.0 copy-start.1
  32.2 0.9 %copy-done.1 = s32[64,4,128]{2,1,0:T(4,128)S(1)} copy-done((s32[64,4,128]{2,1,0:T(4,128)S(1)}, s32[64,4,128]{2,1,0:T(4,128)}, u32[]{:S(2)}) %copy-start.1) | copy-done | bytes 131096
  33.1 19.9 %shard_map.86 = (f32[32,256,128]{2,1,0:T(8,128)S(1)}, f32[64,128,256]{2,1,0:T(8,128)S(1)}) custom-call(s32[1,640]{1,0:T(1,128)S(1)} %get-tuple-element.11.list_ref, s32[64,4,128]{2,1,0:T(4,128)S(1)} %copy-done.1, bf16[4096,256]{1,0:T(8,128)(2,1)S(1)} %get-tuple-element.12.d_ref, bf16[8192,256]{1,0:T(8,128)(2,1)S(1)} %get-tuple-element.13.g_ref, ...), custom_call_target="tpu_custom_call" | custom-call | tf_op jit(solution)/shard_map/pallas_call | solution.py:333
  53.0 33.8 %shard_map.87 = f32[512,256]{1,0:T(8,128)S(1)} custom-call(f32[32,256,128]{2,1,0:T(8,128)S(1)} %get-tuple-element.15.dp_ref, f32[64,128,256]{2,1,0:T(8,128)S(1)} %get-tuple-element.16.sp_ref), custom_call_target="tpu_custom_call" | custom-call | tf_op jit(solution)/shard_map/pallas_call | solution.py:497
  86.7 0.8 copy.10
  (1 shorter events, 0.0 us)
Async XLA Ops:
  1.5 1.0 %copy-start = (bf16[512,256]{1,0:T(8,128)(2,1)S(1)}, bf16[512,256]{1,0:T(8,128)(2,1)}, u32[]{:S(2)}) copy-start(bf16[512,256]{1,0:T(8,128)(2,1)} %e_ref.1) | copy-start | bytes 786436
  32.2 0.9 %copy-start.1 = (s32[64,4,128]{2,1,0:T(4,128)S(1)}, s32[64,4,128]{2,1,0:T(4,128)}, u32[]{:S(2)}) copy-start(s32[64,4,128]{2,1,0:T(4,128)} %bank_ref.1) | copy-start | bytes 393220

commit v8 on v7

--- a/solution.py
+++ b/solution.py
@@ -400,7 +400,7 @@
 
     def send_tile(name, h, value, power, out_buf, in_buf, peer):
         height = value.shape[0]
-        q = jnp.round(value * (jnp.exp2(-power) * LEVELS))
+        q = jnp.round((value * jnp.exp2(-power)) * LEVELS)
         out_buf[pl.ds(HEAD + h * height, height), :] = q.astype(jnp.int32).astype(jnp.int16)
         if h == 0:
             out_buf[pl.ds(0, HEAD), :] = (
@@ -413,7 +413,7 @@
 
     def tile_in(buf, h, bound):
         height = (buf.shape[0] - HEAD) // sub
-        return buf[pl.ds(HEAD + h * height, height), :].astype(jnp.float32) * (bound * (1.0 / LEVELS))
+        return buf[pl.ds(HEAD + h * height, height), :].astype(jnp.float32) * (1.0 / LEVELS) * bound
 
     def got(*names):
         for name in names:

time: 87.8 us -> 88.6 us (level)
    pallas_call x1, Pallas kernels: 33.8 us -> 35.1 us  [reduce_sums(): pl.pallas_call(functools.partial(reduce_kernel, scale), out_shape=jax.Sha...]
    pallas_call x1, Pallas kernels: 19.9 us -> 18.9 us  [pair_sums(): pl.pallas_call(pair_kernel, out_shape=(jax.ShapeDtypeStruct((d.shape[0] /...]
where the time goes in v8:
time: 88.6 us; the launch traced here: 87.9 us
  Pallas kernels  83.7 us (94%)
  local copies, waits for them, and re-layouts  2.64 us (3%)
  other arithmetic  1.52 us (2%)
    pallas_call x1, Pallas kernels, reduce_sums(): pl.pallas_call(functools.partial(reduce_kernel, scale), out_shape=jax.Sha...  35.1 us
    pallas_call x1, Pallas kernels, gather(): pl.pallas_call(functools.partial(gather_kernel, stops), out_shape=(jax.Sh...  29.7 us
    pallas_call x1, Pallas kernels, pair_sums(): pl.pallas_call(pair_kernel, out_shape=(jax.ShapeDtypeStruct((d.shape[0] /...  18.9 us
    unnamed x5, local copies, waits for them, and re-layouts  2.64 us

profile of v8, /device:TPU:1, one launch (start us, length us, event | category | flops | bytes accessed | tf_op | source)
XLA Modules:
  0.0 87.9 jit_solution(4590032019270697631)
XLA Ops:
  0.0 0.7 or_bitcast_fusion
  0.7 0.8 shift-left_or_fusion
  1.5 0.0 copy-start
  1.5 0.9 %copy-done = bf16[512,256]{1,0:T(8,128)(2,1)S(1)} copy-done((bf16[512,256]{1,0:T(8,128)(2,1)S(1)}, bf16[512,256]{1,0:T(8,128)(2,1)}, u32[]{:S(2)}) %copy-start) | copy-done | bytes 262168
  2.5 29.7 %shard_map.85 = (bf16[4096,256]{1,0:T(8,128)(2,1)S(1)}, bf16[8192,256]{1,0:T(8,128)(2,1)S(1)}, bf16[64,256,128]{2,1,0:T(8,128)(2,1)S(1)}, s32[1,640]{1,0:T(1,128)S(1)}) custom-call(bf16[512,256]{1,0:T(8,128)(2,1)S(1)} %copy-done, s32[1,1,20,24]{3,2,1,0:T(8,128)S(1)} %pad_add_fusion.slot_ref), custom_call_target="tpu_custom_call" | custom-call | tf_op jit(solution)/shard_map/pallas_call | solution.py:242
  32.2 0.0 copy-start.1
  32.2 0.9 %copy-done.1 = s32[64,4,128]{2,1,0:T(4,128)S(1)} copy-done((s32[64,4,128]{2,1,0:T(4,128)S(1)}, s32[64,4,128]{2,1,0:T(4,128)}, u32[]{:S(2)}) %copy-start.1) | copy-done | bytes 131096
  33.1 18.9 %shard_map.86 = (f32[32,256,128]{2,1,0:T(8,128)S(1)}, f32[64,128,256]{2,1,0:T(8,128)S(1)}) custom-call(s32[1,640]{1,0:T(1,128)S(1)} %get-tuple-element.11.list_ref, s32[64,4,128]{2,1,0:T(4,128)S(1)} %copy-done.1, bf16[4096,256]{1,0:T(8,128)(2,1)S(1)} %get-tuple-element.12.d_ref, bf16[8192,256]{1,0:T(8,128)(2,1)S(1)} %get-tuple-element.13.g_ref, ...), custom_call_target="tpu_custom_call" | custom-call | tf_op jit(solution)/shard_map/pallas_call | solution.py:333
  52.0 35.1 %shard_map.87 = f32[512,256]{1,0:T(8,128)S(1)} custom-call(f32[32,256,128]{2,1,0:T(8,128)S(1)} %get-tuple-element.15.dp_ref, f32[64,128,256]{2,1,0:T(8,128)S(1)} %get-tuple-element.16.sp_ref), custom_call_target="tpu_custom_call" | custom-call | tf_op jit(solution)/shard_map/pallas_call | solution.py:497
  87.1 0.8 copy.10
  (1 shorter events, 0.0 us)
Async XLA Ops:
  1.5 1.0 %copy-start = (bf16[512,256]{1,0:T(8,128)(2,1)S(1)}, bf16[512,256]{1,0:T(8,128)(2,1)}, u32[]{:S(2)}) copy-start(bf16[512,256]{1,0:T(8,128)(2,1)} %e_ref.1) | copy-start | bytes 786436
  32.2 0.9 %copy-start.1 = (s32[64,4,128]{2,1,0:T(4,128)S(1)}, s32[64,4,128]{2,1,0:T(4,128)}, u32[]{:S(2)}) copy-start(s32[64,4,128]{2,1,0:T(4,128)} %bank_ref.1) | copy-start | bytes 393220

commit v9 on v8

--- a/solution.py
+++ b/solution.py
@@ -262,13 +262,6 @@
 
 
 def pair_kernel(list_ref, bank_ref, d_ref, g_ref, gt_ref, dp_ref, sp_ref, coded):
-    def clear(i, carry):
-        dp_ref[i] = jnp.zeros(dp_ref.shape[1:], dp_ref.dtype)
-        for k in range(sp_ref.shape[0] // dp_ref.shape[0]):
-            sp_ref[i * (sp_ref.shape[0] // dp_ref.shape[0]) + k] = jnp.zeros(sp_ref.shape[1:], sp_ref.dtype)
-        return carry
-
-    lax.fori_loop(0, dp_ref.shape[0], clear, 0)
     pairs = list_ref[0, list_ref.shape[1] - 1]
     one_bit = jnp.left_shift(1, lax.broadcasted_iota(jnp.int32, (32, T), 0))
 
@@ -310,8 +303,16 @@
         dp_ref[p[0]] += to_dest[:, :T]
         dp_ref[p[1]] += to_dest[:, T:]
 
-    for u in range(UNROLL):
+    def begin(u, carry):
         coded[0, u] = first(u)
+        for ref in (dp_ref, sp_ref):
+            share = ref.shape[0] // UNROLL
+            for k in range(share):
+                ref[u * share + k] = jnp.zeros(ref.shape[1:], ref.dtype)
+        return carry
+
+    assert dp_ref.shape[0] % UNROLL == 0 and sp_ref.shape[0] % UNROLL == 0
+    lax.fori_loop(0, UNROLL, begin, 0)
 
     def body(step, carry):
         now = lax.rem(step, 2)

time: 88.6 us -> 88.1 us (level)
    pallas_call x1, Pallas kernels: 35.1 us -> 32.7 us  [reduce_sums(): pl.pallas_call(functools.partial(reduce_kernel, scale), out_shape=jax.Sha...]
    pallas_call x1, Pallas kernels: 18.9 us -> 21.3 us  [pair_sums(): pl.pallas_call(pair_kernel, out_shape=(jax.ShapeDtypeStruct((d.shape[0] /...]
where the time goes in v9:
time: 88.1 us; the launch traced here: 87.8 us
  Pallas kernels  83.6 us (95%)
  local copies, waits for them, and re-layouts  2.64 us (3%)
  other arithmetic  1.52 us (2%)
    pallas_call x1, Pallas kernels, reduce_sums(): pl.pallas_call(functools.partial(reduce_kernel, scale), out_shape=jax.Sha...  32.7 us
    pallas_call x1, Pallas kernels, gather(): pl.pallas_call(functools.partial(gather_kernel, stops), out_shape=(jax.Sh...  29.7 us
    pallas_call x1, Pallas kernels, pair_sums(): pl.pallas_call(pair_kernel, out_shape=(jax.ShapeDtypeStruct((d.shape[0] /...  21.3 us
    unnamed x5, local copies, waits for them, and re-layouts  2.64 us

profile of v9, /device:TPU:1, one launch (start us, length us, event | category | flops | bytes accessed | tf_op | source)
XLA Modules:
  0.0 87.8 jit_solution(12168677112998861020)
XLA Ops:
  0.0 0.7 or_bitcast_fusion
  0.7 0.8 shift-left_or_fusion
  1.5 0.0 copy-start
  1.5 0.9 %copy-done = bf16[512,256]{1,0:T(8,128)(2,1)S(1)} copy-done((bf16[512,256]{1,0:T(8,128)(2,1)S(1)}, bf16[512,256]{1,0:T(8,128)(2,1)}, u32[]{:S(2)}) %copy-start) | copy-done | bytes 262168
  2.5 29.7 %shard_map.85 = (bf16[4096,256]{1,0:T(8,128)(2,1)S(1)}, bf16[8192,256]{1,0:T(8,128)(2,1)S(1)}, bf16[64,256,128]{2,1,0:T(8,128)(2,1)S(1)}, s32[1,640]{1,0:T(1,128)S(1)}) custom-call(bf16[512,256]{1,0:T(8,128)(2,1)S(1)} %copy-done, s32[1,1,20,24]{3,2,1,0:T(8,128)S(1)} %pad_add_fusion.slot_ref), custom_call_target="tpu_custom_call" | custom-call | tf_op jit(solution)/shard_map/pallas_call | solution.py:242
  32.2 0.0 copy-start.1
  32.2 0.9 %copy-done.1 = s32[64,4,128]{2,1,0:T(4,128)S(1)} copy-done((s32[64,4,128]{2,1,0:T(4,128)S(1)}, s32[64,4,128]{2,1,0:T(4,128)}, u32[]{:S(2)}) %copy-start.1) | copy-done | bytes 131096
  33.1 21.3 %shard_map.86 = (f32[32,256,128]{2,1,0:T(8,128)S(1)}, f32[64,128,256]{2,1,0:T(8,128)S(1)}) custom-call(s32[1,640]{1,0:T(1,128)S(1)} %get-tuple-element.11.list_ref, s32[64,4,128]{2,1,0:T(4,128)S(1)} %copy-done.1, bf16[4096,256]{1,0:T(8,128)(2,1)S(1)} %get-tuple-element.12.d_ref, bf16[8192,256]{1,0:T(8,128)(2,1)S(1)} %get-tuple-element.13.g_ref, ...), custom_call_target="tpu_custom_call" | custom-call | tf_op jit(solution)/shard_map/pallas_call | solution.py:334
  54.4 32.7 %shard_map.87 = f32[512,256]{1,0:T(8,128)S(1)} custom-call(f32[32,256,128]{2,1,0:T(8,128)S(1)} %get-tuple-element.15.dp_ref, f32[64,128,256]{2,1,0:T(8,128)S(1)} %get-tuple-element.16.sp_ref), custom_call_target="tpu_custom_call" | custom-call | tf_op jit(solution)/shard_map/pallas_call | solution.py:498
  87.0 0.8 copy.10
  (1 shorter events, 0.0 us)
Async XLA Ops:
  1.5 1.0 %copy-start = (bf16[512,256]{1,0:T(8,128)(2,1)S(1)}, bf16[512,256]{1,0:T(8,128)(2,1)}, u32[]{:S(2)}) copy-start(bf16[512,256]{1,0:T(8,128)(2,1)} %e_ref.1) | copy-start | bytes 786436
  32.2 0.9 %copy-start.1 = (s32[64,4,128]{2,1,0:T(4,128)S(1)}, s32[64,4,128]{2,1,0:T(4,128)}, u32[]{:S(2)}) copy-start(s32[64,4,128]{2,1,0:T(4,128)} %bank_ref.1) | copy-start | bytes 393220

commit v10 on v8

--- a/solution.py
+++ b/solution.py
@@ -262,13 +262,6 @@
 
 
 def pair_kernel(list_ref, bank_ref, d_ref, g_ref, gt_ref, dp_ref, sp_ref, coded):
-    def clear(i, carry):
-        dp_ref[i] = jnp.zeros(dp_ref.shape[1:], dp_ref.dtype)
-        for k in range(sp_ref.shape[0] // dp_ref.shape[0]):
-            sp_ref[i * (sp_ref.shape[0] // dp_ref.shape[0]) + k] = jnp.zeros(sp_ref.shape[1:], sp_ref.dtype)
-        return carry
-
-    lax.fori_loop(0, dp_ref.shape[0], clear, 0)
     pairs = list_ref[0, list_ref.shape[1] - 1]
     one_bit = jnp.left_shift(1, lax.broadcasted_iota(jnp.int32, (32, T), 0))
 
@@ -312,6 +305,9 @@
 
     for u in range(UNROLL):
         coded[0, u] = first(u)
+        for ref in (dp_ref, sp_ref):
+            for tile in range(u, ref.shape[0], UNROLL):
+                ref[tile] = jnp.zeros(ref.shape[1:], ref.dtype)
 
     def body(step, carry):
         now = lax.rem(step, 2)

time: 88.6 us -> 88.7 us (level); the launches traced: 87.9 us -> 89.1 us
  Pallas kernels: 83.7 us -> 84.9 us
    pallas_call x1, Pallas kernels: 35.1 us -> 37.3 us  [reduce_sums(): pl.pallas_call(functools.partial(reduce_kernel, scale), out_shape=jax.Sha...]
    pallas_call x1, Pallas kernels: 18.9 us -> 17.9 us  [pair_sums(): pl.pallas_call(pair_kernel, out_shape=(jax.ShapeDtypeStruct((d.shape[0] /...]
where the time goes in v10:
time: 88.7 us; the launch traced here: 89.1 us
  Pallas kernels  84.9 us (96%)
  local copies, waits for them, and re-layouts  2.64 us (3%)
  other arithmetic  1.52 us (2%)
    pallas_call x1, Pallas kernels, reduce_sums(): pl.pallas_call(functools.partial(reduce_kernel, scale), out_shape=jax.Sha...  37.3 us
    pallas_call x1, Pallas kernels, gather(): pl.pallas_call(functools.partial(gather_kernel, stops), out_shape=(jax.Sh...  29.7 us
    pallas_call x1, Pallas kernels, pair_sums(): pl.pallas_call(pair_kernel, out_shape=(jax.ShapeDtypeStruct((d.shape[0] /...  17.9 us
    unnamed x5, local copies, waits for them, and re-layouts  2.64 us

profile of v10, /device:TPU:1, one launch (start us, length us, event | category | flops | bytes accessed | tf_op | source)
XLA Modules:
  0.0 89.1 jit_solution(335537336375974596)
XLA Ops:
  0.0 0.7 or_bitcast_fusion
  0.7 0.8 shift-left_or_fusion
  1.5 0.0 copy-start
  1.5 0.9 %copy-done = bf16[512,256]{1,0:T(8,128)(2,1)S(1)} copy-done((bf16[512,256]{1,0:T(8,128)(2,1)S(1)}, bf16[512,256]{1,0:T(8,128)(2,1)}, u32[]{:S(2)}) %copy-start) | copy-done | bytes 262168
  2.5 29.7 %shard_map.85 = (bf16[4096,256]{1,0:T(8,128)(2,1)S(1)}, bf16[8192,256]{1,0:T(8,128)(2,1)S(1)}, bf16[64,256,128]{2,1,0:T(8,128)(2,1)S(1)}, s32[1,640]{1,0:T(1,128)S(1)}) custom-call(bf16[512,256]{1,0:T(8,128)(2,1)S(1)} %copy-done, s32[1,1,20,24]{3,2,1,0:T(8,128)S(1)} %pad_add_fusion.slot_ref), custom_call_target="tpu_custom_call" | custom-call | tf_op jit(solution)/shard_map/pallas_call | solution.py:242
  32.2 0.0 copy-start.1
  32.2 0.9 %copy-done.1 = s32[64,4,128]{2,1,0:T(4,128)S(1)} copy-done((s32[64,4,128]{2,1,0:T(4,128)S(1)}, s32[64,4,128]{2,1,0:T(4,128)}, u32[]{:S(2)}) %copy-start.1) | copy-done | bytes 131096
  33.1 17.9 %shard_map.86 = (f32[32,256,128]{2,1,0:T(8,128)S(1)}, f32[64,128,256]{2,1,0:T(8,128)S(1)}) custom-call(s32[1,640]{1,0:T(1,128)S(1)} %get-tuple-element.11.list_ref, s32[64,4,128]{2,1,0:T(4,128)S(1)} %copy-done.1, bf16[4096,256]{1,0:T(8,128)(2,1)S(1)} %get-tuple-element.12.d_ref, bf16[8192,256]{1,0:T(8,128)(2,1)S(1)} %get-tuple-element.13.g_ref, ...), custom_call_target="tpu_custom_call" | custom-call | tf_op jit(solution)/shard_map/pallas_call | solution.py:329
  51.0 37.3 %shard_map.87 = f32[512,256]{1,0:T(8,128)S(1)} custom-call(f32[32,256,128]{2,1,0:T(8,128)S(1)} %get-tuple-element.15.dp_ref, f32[64,128,256]{2,1,0:T(8,128)S(1)} %get-tuple-element.16.sp_ref), custom_call_target="tpu_custom_call" | custom-call | tf_op jit(solution)/shard_map/pallas_call | solution.py:493
  88.3 0.8 copy.10
  (1 shorter events, 0.0 us)
Async XLA Ops:
  1.5 1.0 %copy-start = (bf16[512,256]{1,0:T(8,128)(2,1)S(1)}, bf16[512,256]{1,0:T(8,128)(2,1)}, u32[]{:S(2)}) copy-start(bf16[512,256]{1,0:T(8,128)(2,1)} %e_ref.1) | copy-start | bytes 786436
  32.2 0.9 %copy-start.1 = (s32[64,4,128]{2,1,0:T(4,128)S(1)}, s32[64,4,128]{2,1,0:T(4,128)}, u32[]{:S(2)}) copy-start(s32[64,4,128]{2,1,0:T(4,128)} %bank_ref.1) | copy-start | bytes 393220
